TPU v7x, 32 devices: a whole 2x2x4 slice. The times are simulated.
32 devices in a mesh: dp: 8 (over y, x, core), sp: 4 (over z).
Axes of the slice: x: 2, y: 2, z: 4, core: 2. Of those that a mesh axis runs over, the one named last changes fastest.
Arguments:
- tokens: bfloat16 [8, 4096, 768], P('dp', 'sp'), may hold values from -6 to 6
- qkv_weight: bfloat16 [768, 2304], P(('dp', 'sp')), may hold values from -0.21875 to 0.21875
- query_value_bias: bfloat16 [2, 768], P(None, ('dp', 'sp')), may hold values from -3 to 3
- out_weight: bfloat16 [768, 768], P(('dp', 'sp')), may hold values from -1.75 to 1.75
- out_bias: bfloat16 [768], P(('dp', 'sp')), may hold values from -3 to 3
- norm1_gain: bfloat16 [768], P(('dp', 'sp')), may hold values from 0.099609375 to 1.8984375
- norm1_bias: bfloat16 [768], P(('dp', 'sp')), may hold values from -3 to 3
- up_weight: bfloat16 [768, 3072], P(('dp', 'sp')), may hold values from -0.21875 to 0.21875
- up_bias: bfloat16 [3072], P(('dp', 'sp')), may hold values from -3 to 3
- down_weight: bfloat16 [3072, 768], P(('dp', 'sp')), may hold values from -0.109375 to 0.109375
- down_bias: bfloat16 [768], P(('dp', 'sp')), may hold values from -3 to 3
- norm2_gain: bfloat16 [768], P(('dp', 'sp')), may hold values from 0.099609375 to 1.8984375
- norm2_bias: bfloat16 [768], P(('dp', 'sp')), may hold values from -3 to 3
- rand_blocks: int32 [8, 12, 62, 3], P('dp', 'sp'), may hold values from 1 to 62, as said below
- out_grad: bfloat16 [8, 4096, 768], P('dp', 'sp'), may hold values from -6 to 6
Outputs:
- layer_out: bfloat16 [8, 4096, 768], P('dp', 'sp')
- input_grad: float32 [8, 4096, 768], P('dp', 'sp')
- qkv_weight_grad: float32 [768, 2304], P(('dp', 'sp'))
- query_value_bias_grad: float32 [2, 768], P(None, ('dp', 'sp'))
- out_weight_grad: float32 [768, 768], P(('dp', 'sp'))
- out_bias_grad: float32 [768], P(('dp', 'sp'))
- norm1_gain_grad: float32 [768], P(('dp', 'sp'))
- norm1_bias_grad: float32 [768], P(('dp', 'sp'))
- up_weight_grad: float32 [768, 3072], P(('dp', 'sp'))
- up_bias_grad: float32 [3072], P(('dp', 'sp'))
- down_weight_grad: float32 [3072, 768], P(('dp', 'sp'))
- down_bias_grad: float32 [768], P(('dp', 'sp'))
- norm2_gain_grad: float32 [768], P(('dp', 'sp'))
- norm2_bias_grad: float32 [768], P(('dp', 'sp'))
Inputs may be any that keep to these rules, and one draw needn't show every extreme that they name: For middle query block i, the 3 entries of rand_blocks[b, h, i - 1] are distinct and none of them is i - 1, i, i + 1, 0 or 63.
All inputs are finite; a program needn't handle non-finite values.
Results may differ from a plain program's by a relative error of at most 0.013.
Values may be sent and summed in bfloat16 or wider, within the bound.
A program may use at most 256 MiB of HBM per device.

v0:
```python
from functools import partial

import jax
import jax.numpy as jnp
from jax import lax
from jax.sharding import PartitionSpec as P

HEAD_DIM = 64
BLOCK = 64


norm_eps = 1e-05
masked_score = -1e30
highest_mode = lax.Precision.HIGHEST


def middle_mask(blocks, slots, width):
    position = jnp.arange(1, blocks - 1, dtype=jnp.int32)[:, None]
    column = jnp.arange(slots, dtype=jnp.int32)[None, :]
    marks = (position == 1) & (column == 3) | (position == blocks - 2) & (column == 4)
    return jnp.repeat(marks, width, axis=1)


def listed_pair(keys_in, values_in, rand_head):
    blocks, width, head_width = keys_in.shape
    middle = blocks - 2
    pair = jnp.stack([keys_in, values_in])
    window = jnp.stack(
        [pair[:, 0:middle], pair[:, 1 : middle + 1], pair[:, 2 : middle + 2]], axis=2
    )
    ends = jnp.stack([pair[:, 0], pair[:, blocks - 1]], axis=1)
    ends = jnp.broadcast_to(ends[:, None], (2, middle, 2, width, head_width))
    remote = pair[:, rand_head]
    listed = jnp.concatenate([window, ends, remote], axis=2)
    return listed.reshape(2, middle, -1, head_width)


def normalize(resid, gain, shift):
    center = resid - jnp.mean(resid, axis=1, keepdims=True)
    rstd = lax.rsqrt(jnp.mean(center * center, axis=1, keepdims=True) + norm_eps)
    normed = center * rstd
    return (normed * gain + shift, normed, rstd)


def normalize_back(upstream, normed, rstd, gain):
    gain_grad = jnp.sum(upstream * normed, axis=0)
    shift_grad = jnp.sum(upstream, axis=0)
    dnormed = upstream * gain
    dresid = rstd * (
        dnormed
        - jnp.mean(dnormed, axis=1, keepdims=True)
        - normed * jnp.mean(dnormed * normed, axis=1, keepdims=True)
    )
    return (dresid, gain_grad, shift_grad)


def middle_scores(queries, listed, rand_head):
    blocks, width, head_width = queries.shape
    score_scale_factor = head_width ** (-0.5)
    raw_scores = score_scale_factor * jnp.einsum(
        "mif,mcf->mic", queries[1:-1], listed[0], preferred_element_type=jnp.float32
    )
    masks = middle_mask(blocks, 5 + rand_head.shape[1], width)
    return jnp.where(masks[:, None, :], jnp.full_like(raw_scores, masked_score), raw_scores)


def head_forward(queries, keys_in, values_in, rand_head):
    blocks, width, head_width = queries.shape
    score_scale_factor = head_width ** (-0.5)
    listed = listed_pair(keys_in, values_in, rand_head)
    scores = middle_scores(queries, listed, rand_head)
    log_total = jax.nn.logsumexp(scores, axis=2)
    attn_probs = jnp.exp(scores - log_total[:, :, None]).astype(jnp.bfloat16)
    mid_out = jnp.einsum("mic,mcf->mif", attn_probs, listed[1], preferred_element_type=jnp.float32)
    flat_keys = keys_in.reshape(-1, head_width)
    flat_values = values_in.reshape(-1, head_width)
    global_rows = jnp.concatenate([queries[0], queries[blocks - 1]], axis=0)
    glob_scores = score_scale_factor * jnp.einsum(
        "qf,tf->qt", global_rows, flat_keys, preferred_element_type=jnp.float32
    )
    glob_total = jax.nn.logsumexp(glob_scores, axis=1)
    glob_probs = jnp.exp(glob_scores - glob_total[:, None]).astype(jnp.bfloat16)
    glob_out = jnp.dot(glob_probs, flat_values, preferred_element_type=jnp.float32)
    context = jnp.concatenate([glob_out[:width][None], mid_out, glob_out[width:][None]], axis=0)
    log_totals = jnp.concatenate(
        [glob_total[:width][None], log_total, glob_total[width:][None]], axis=0
    )
    return (context.astype(jnp.bfloat16), log_totals)


def head_backward(queries, keys_in, values_in, rand_head, log_totals, dcontext):
    blocks, width, head_width = queries.shape
    middle = blocks - 2
    score_scale_factor = head_width ** (-0.5)
    listed = listed_pair(keys_in, values_in, rand_head)
    scores = middle_scores(queries, listed, rand_head)
    attn_probs = jnp.exp(scores - log_totals[1:-1][:, :, None])
    probs_low = attn_probs.astype(jnp.bfloat16)
    grad_mid = dcontext[1:-1]
    query_mid = queries[1:-1]
    dprob = jnp.einsum("mif,mcf->mic", grad_mid, listed[1], preferred_element_type=jnp.float32)
    delta = jnp.sum(attn_probs * dprob, axis=2, keepdims=True)
    dscore = (attn_probs * (dprob - delta)).astype(jnp.bfloat16)
    dquery_mid = score_scale_factor * jnp.einsum(
        "mic,mcf->mif", dscore, listed[0], preferred_element_type=jnp.float32
    )
    dkey_list = score_scale_factor * jnp.einsum(
        "mic,mif->mcf", dscore, query_mid, preferred_element_type=jnp.float32
    )
    dvalue_list = jnp.einsum(
        "mic,mif->mcf", probs_low, grad_mid, preferred_element_type=jnp.float32
    )
    slot_grads = jnp.stack([dkey_list, dvalue_list]).reshape(2, middle, -1, width, head_width)
    edges = ((0, 0),)
    tail = ((0, 0), (0, 0))
    pair_total = jnp.pad(slot_grads[:, :, 0], edges + ((0, 2),) + tail)
    pair_total = pair_total + jnp.pad(slot_grads[:, :, 1], edges + ((1, 1),) + tail)
    pair_total = pair_total + jnp.pad(slot_grads[:, :, 2], edges + ((2, 0),) + tail)
    pair_total = pair_total.at[:, 0].add(jnp.sum(slot_grads[:, :, 3], axis=1))
    pair_total = pair_total.at[:, blocks - 1].add(jnp.sum(slot_grads[:, :, 4], axis=1))
    onehot = (rand_head[:, :, None] == jnp.arange(blocks, dtype=jnp.int32)[None, None, :]).astype(
        jnp.float32
    )
    pair_total = pair_total + jnp.einsum(
        "mrn,smrif->snif", onehot, slot_grads[:, :, 5:], precision=highest_mode
    )
    flat_keys = keys_in.reshape(-1, head_width)
    flat_values = values_in.reshape(-1, head_width)
    global_rows = jnp.concatenate([queries[0], queries[blocks - 1]], axis=0)
    global_grads = jnp.concatenate([dcontext[0], dcontext[blocks - 1]], axis=0)
    glob_totals = jnp.concatenate([log_totals[0], log_totals[blocks - 1]], axis=0)
    glob_scores = score_scale_factor * jnp.einsum(
        "qf,tf->qt", global_rows, flat_keys, preferred_element_type=jnp.float32
    )
    glob_probs = jnp.exp(glob_scores - glob_totals[:, None])
    glob_low = glob_probs.astype(jnp.bfloat16)
    glob_dprob = jnp.einsum(
        "qf,tf->qt", global_grads, flat_values, preferred_element_type=jnp.float32
    )
    glob_delta = jnp.sum(glob_probs * glob_dprob, axis=1, keepdims=True)
    glob_dscore = (glob_probs * (glob_dprob - glob_delta)).astype(jnp.bfloat16)
    glob_dquery = score_scale_factor * jnp.dot(
        glob_dscore, flat_keys, preferred_element_type=jnp.float32
    )
    key_total = pair_total[0].reshape(-1, head_width) + score_scale_factor * jnp.einsum(
        "qt,qf->tf", glob_dscore, global_rows, preferred_element_type=jnp.float32
    )
    value_total = pair_total[1].reshape(-1, head_width) + jnp.einsum(
        "qt,qf->tf", glob_low, global_grads, preferred_element_type=jnp.float32
    )
    dquery = jnp.concatenate(
        [glob_dquery[:width][None], dquery_mid, glob_dquery[width:][None]], axis=0
    )
    shape = (blocks, width, head_width)
    return (
        dquery.astype(jnp.bfloat16),
        key_total.reshape(shape).astype(jnp.bfloat16),
        value_total.reshape(shape).astype(jnp.bfloat16),
    )


def per_device(
    tokens,
    qkv_weight,
    query_value_bias,
    out_weight,
    out_bias,
    norm1_gain,
    norm1_bias,
    up_weight,
    up_bias,
    down_weight,
    down_bias,
    norm2_gain,
    norm2_bias,
    rand_blocks,
    out_grad,
):
    seq_groups = lax.axis_size("sp")
    gathered = (
        lax.all_gather(qkv_weight, ("dp", "sp"), axis=0, tiled=True),
        lax.all_gather(query_value_bias, ("dp", "sp"), axis=1, tiled=True),
        lax.all_gather(out_weight, ("dp", "sp"), axis=0, tiled=True),
        lax.all_gather(out_bias, ("dp", "sp"), axis=0, tiled=True),
        lax.all_gather(norm1_gain, ("dp", "sp"), axis=0, tiled=True),
        lax.all_gather(norm1_bias, ("dp", "sp"), axis=0, tiled=True),
        lax.all_gather(up_weight, ("dp", "sp"), axis=0, tiled=True),
        lax.all_gather(up_bias, ("dp", "sp"), axis=0, tiled=True),
        lax.all_gather(down_weight, ("dp", "sp"), axis=0, tiled=True),
        lax.all_gather(down_bias, ("dp", "sp"), axis=0, tiled=True),
        lax.all_gather(norm2_gain, ("dp", "sp"), axis=0, tiled=True),
        lax.all_gather(norm2_bias, ("dp", "sp"), axis=0, tiled=True),
    )
    attn_set = gathered[:6]
    ffn_set = gathered[6:]
    w_qkv, bias_pair, w_proj, bias_proj, gain_first, shift_first = attn_set
    inputs = tokens[0]
    local_rows, model_width = inputs.shape
    rand_dev = rand_blocks[0]
    heads_dev = rand_dev.shape[0]
    head_cols = heads_dev * HEAD_DIM
    bias_cols = jnp.concatenate(
        [bias_pair[0], jnp.zeros((model_width,), jnp.bfloat16), bias_pair[1]]
    ).astype(jnp.float32)
    raw = jnp.dot(inputs, w_qkv, preferred_element_type=jnp.float32) + bias_cols[None, :]
    packed = raw.astype(jnp.bfloat16).reshape(local_rows, 3, seq_groups, head_cols)
    arrived = lax.all_to_all(packed, "sp", split_axis=2, concat_axis=0, tiled=True)
    length = arrived.shape[0]
    blocks = length // BLOCK
    heads = jnp.transpose(arrived.reshape(blocks, BLOCK, 3, heads_dev, HEAD_DIM), (2, 3, 0, 1, 4))
    context_heads, log_totals = lax.map(
        lambda operands: head_forward(*operands), (heads[0], heads[1], heads[2], rand_dev)
    )
    context_send = jnp.transpose(context_heads, (1, 2, 0, 3)).reshape(
        seq_groups, local_rows, head_cols
    )
    context = lax.all_to_all(context_send, "sp", split_axis=0, concat_axis=2, tiled=True).reshape(
        local_rows, model_width
    )
    attn_proj = jnp.dot(context, w_proj, preferred_element_type=jnp.float32) + bias_proj.astype(
        jnp.float32
    )
    inputs_wide = inputs.astype(jnp.float32)
    gain_one = gain_first.astype(jnp.float32)
    hidden1, normed1, rstd1 = normalize(
        inputs_wide + attn_proj, gain_one, shift_first.astype(jnp.float32)
    )
    w_up, bias_up, w_down, bias_down, gain_second, shift_second = ffn_set
    hidden_low = hidden1.astype(jnp.bfloat16)
    pre = jnp.dot(hidden_low, w_up, preferred_element_type=jnp.float32) + bias_up.astype(
        jnp.float32
    )
    act, gelu_back = jax.vjp(partial(jax.nn.gelu, approximate=True), pre)
    act_low = act.astype(jnp.bfloat16)
    ffn_out = jnp.dot(act_low, w_down, preferred_element_type=jnp.float32) + bias_down.astype(
        jnp.float32
    )
    gain_two = gain_second.astype(jnp.float32)
    result, normed2, rstd2 = normalize(
        hidden1 + ffn_out, gain_two, shift_second.astype(jnp.float32)
    )
    upstream = out_grad[0].astype(jnp.float32)
    dresid2, gain2_grad, shift2_grad = normalize_back(upstream, normed2, rstd2, gain_two)
    dffn = dresid2.astype(jnp.bfloat16)
    down_grad = jnp.einsum("tf,td->fd", act_low, dffn, preferred_element_type=jnp.float32)
    down_bias_grad = jnp.sum(dffn, axis=0, dtype=jnp.float32)
    dact = jnp.einsum("td,fd->tf", dffn, w_down, preferred_element_type=jnp.float32)
    dpre = gelu_back(dact)[0].astype(jnp.bfloat16)
    up_grad = jnp.einsum("td,tf->df", hidden_low, dpre, preferred_element_type=jnp.float32)
    up_bias_grad = jnp.sum(dpre, axis=0, dtype=jnp.float32)
    dhidden1 = dresid2 + jnp.einsum("tf,df->td", dpre, w_up, preferred_element_type=jnp.float32)
    dresid1, gain1_grad, shift1_grad = normalize_back(dhidden1, normed1, rstd1, gain_one)
    dproj = dresid1.astype(jnp.bfloat16)
    proj_grad = jnp.einsum("tc,td->cd", context, dproj, preferred_element_type=jnp.float32)
    proj_bias_grad = jnp.sum(dproj, axis=0, dtype=jnp.float32)
    dcontext = jnp.einsum("td,cd->tc", dproj, w_proj, preferred_element_type=jnp.float32).astype(
        jnp.bfloat16
    )
    dcontext_send = dcontext.reshape(local_rows, seq_groups, head_cols)
    dcontext_heads = lax.all_to_all(dcontext_send, "sp", split_axis=1, concat_axis=0, tiled=True)
    dheads = jnp.transpose(dcontext_heads.reshape(blocks, BLOCK, heads_dev, HEAD_DIM), (2, 0, 1, 3))
    dquery, dkey, dvalue = lax.map(
        lambda operands: head_backward(*operands),
        (heads[0], heads[1], heads[2], rand_dev, log_totals, dheads),
    )
    grad_heads = jnp.transpose(jnp.stack([dquery, dkey, dvalue]), (2, 3, 0, 1, 4)).reshape(
        seq_groups, local_rows, 3, 1, head_cols
    )
    grad_cols = lax.all_to_all(grad_heads, "sp", split_axis=0, concat_axis=3, tiled=True).reshape(
        local_rows, 3 * model_width
    )
    input_grad = dresid1 + jnp.einsum(
        "tc,dc->td", grad_cols, w_qkv, preferred_element_type=jnp.float32
    )
    qkv_grad = jnp.einsum("td,tc->dc", inputs, grad_cols, preferred_element_type=jnp.float32)
    col_sums = jnp.sum(grad_cols, axis=0, dtype=jnp.float32)
    pair_grad = jnp.stack([col_sums[:model_width], col_sums[2 * model_width :]])
    summed = (
        lax.psum_scatter(qkv_grad, ("dp", "sp"), scatter_dimension=0, tiled=True),
        lax.psum_scatter(pair_grad, ("dp", "sp"), scatter_dimension=1, tiled=True),
        lax.psum_scatter(proj_grad, ("dp", "sp"), scatter_dimension=0, tiled=True),
        lax.psum_scatter(proj_bias_grad, ("dp", "sp"), scatter_dimension=0, tiled=True),
        lax.psum_scatter(gain1_grad, ("dp", "sp"), scatter_dimension=0, tiled=True),
        lax.psum_scatter(shift1_grad, ("dp", "sp"), scatter_dimension=0, tiled=True),
        lax.psum_scatter(up_grad, ("dp", "sp"), scatter_dimension=0, tiled=True),
        lax.psum_scatter(up_bias_grad, ("dp", "sp"), scatter_dimension=0, tiled=True),
        lax.psum_scatter(down_grad, ("dp", "sp"), scatter_dimension=0, tiled=True),
        lax.psum_scatter(down_bias_grad, ("dp", "sp"), scatter_dimension=0, tiled=True),
        lax.psum_scatter(gain2_grad, ("dp", "sp"), scatter_dimension=0, tiled=True),
        lax.psum_scatter(shift2_grad, ("dp", "sp"), scatter_dimension=0, tiled=True),
    )
    return (
        result[None].astype(jnp.bfloat16),
        input_grad[None],
        summed[0],
        summed[1],
        summed[2],
        summed[3],
        summed[4],
        summed[5],
        summed[6],
        summed[7],
        summed[8],
        summed[9],
        summed[10],
        summed[11],
    )


def solution(mesh):
    placed = (
        P("dp", "sp", None),
        P(("dp", "sp"), None),
        P(None, ("dp", "sp")),
        P(("dp", "sp"), None),
        P(("dp", "sp")),
        P(("dp", "sp")),
        P(("dp", "sp")),
        P(("dp", "sp"), None),
        P(("dp", "sp")),
        P(("dp", "sp"), None),
        P(("dp", "sp")),
        P(("dp", "sp")),
        P(("dp", "sp")),
        P("dp", "sp", None, None),
        P("dp", "sp", None),
    )
    return jax.shard_map(
        per_device,
        mesh=mesh,
        in_specs=placed,
        out_specs=(
            P("dp", "sp", None),
            P("dp", "sp", None),
            P(("dp", "sp"), None),
            P(None, ("dp", "sp")),
            P(("dp", "sp"), None),
            P(("dp", "sp")),
            P(("dp", "sp")),
            P(("dp", "sp")),
            P(("dp", "sp"), None),
            P(("dp", "sp")),
            P(("dp", "sp"), None),
            P(("dp", "sp")),
            P(("dp", "sp")),
            P(("dp", "sp")),
        ),
        check_vma=False,
    )
```

profile of v0, /device:TPU:0, one launch (start us, length us, event | category | flops | bytes accessed | tf_op | source)
XLA Modules:
  0.0 1717.8 jit_solution(11068495372316280503)
XLA Ops:
  9.4 69.5 %all-gather = bf16[32,24,2]{1,2,0:T(2,128)(2,1)S(1)} all-gather(bf16[1,24,2]{1,2,0:T(2,128)(2,1)} %bitcast.386), channel_id=1, replica_groups=mesh['dp'=8,'sp'=4] {'dp','sp'}, dimensions={0}, use_global_device_ids=true | all-gather | bytes 3168 | tf_op jit(solution)/shard_map/all_gather | solution.py:182
  105.1 107.0 %all-to-all-done = bf16[1024,3,4,192]{0,3,1,2:T(8,128)(2,1)} async-done(((bf16[1024,3,4,192]{0,3,1,2:T(8,128)(2,1)}), bf16[1024,3,4,192]{0,3,1,2:T(8,128)(2,1)}, u32[]{:S(2)}, u32[]{:S(2)}) %all-to-all-start) | async-done | bytes 4718624 | tf_op jit(solution)/shard_map/all_to_all | solution.py:207
  220.3 13.4 reshape.553
  256.0 194.2 %while.30 = (s32[]{:T(128)}, bf16[3,64,64,64]{3,2,1,0:T(8,128)(2,1)}, f32[3,64,64]{2,1,0:T(8,128)S(1)}, bf16[3,64,64,64]{3,2,1,0:T(8,128)(2,1)}, bf16[3,64,64,64...) while((s32[]{:T(128)}, ...), condition=%wide.region_5.6_spmd, body=%wide.region_0.5_spmd.sunk | while | flops 683781312 | bytes 122038000 | solution.py:211
  297.3 14.3 fusion.200
  358.3 14.3 fusion.200
  419.1 14.3 fusion.200
  468.6 52.8 %all-reduce.19 = (bf16[768]{0:T(1024)(128)(2,1)S(1)}, bf16[768]{0:T(1024)(128)(2,1)S(1)}, bf16[768]{0:T(1024)(128)(2,1)S(1)}, bf16[768]{0:T(1024)(128)(2,1)S(1)}...) all-reduce(bf16[768]{0:T(1024)(128)(2,1)S(1)} %dynamic-update-slice, ...), channel_id=1, replica_groups=mesh['dp'=8,'sp'=4] {'dp','sp'}, use_global_device_ids=true, to_apply=%add.3 | all-reduce | flops 7680 | bytes 30720
  556.0 17.7 %convert_reduce_fusion = (f32[3072]{0:T(1024)}, bf16[1024,3072]{1,0:T(8,128)(2,1)}) fusion(f32[1024,3072]{1,0:T(8,128)} %fusion.104, f32[3072]{0:T(1024)S(1)} %convert_element_type.174, bf16[1024,768]{0,1:T(8,128)(2,1)S(1)} %get-tuple-element.475, bf16[3072,768]{1,0:T(8,128)(2,1)S(1)} %bitcast.388), kind=kOutput, calls=%fused_computation.196 | convolution fusion | flops 4904186880 | bytes 25190400 | tf_op jit(solution)/shard_map/td,fd->tf/dot_general | solution.py:247
  590.8 14.4 fusion.106
  625.2 32.2 %all-to-all-done.2 = bf16[1024,4,192]{0,2,1:T(8,128)(2,1)} async-done(((bf16[1024,4,192]{0,2,1:T(8,128)(2,1)}), bf16[1024,4,192]{0,2,1:T(8,128)(2,1)}, u32[]{:S(2)}, u32[]{:S(2)}) %all-to-all-start.2) | async-done | bytes 1572896 | tf_op jit(solution)/shard_map/all_to_all | solution.py:260
  663.3 776.2 %while.31 = (s32[]{:T(128)}, bf16[3,64,64,64]{2,1,3,0:T(8,128)(2,1)}, bf16[3,64,64,64]{2,1,3,0:T(8,128)(2,1)}, bf16[3,64,64,64]{2,1,3,0:T(8,128)(2,1)}, bf16[3,6...) while((s32[]{:T(128)}, ...), condition=%wide.region_19.20_spmd, body=%wide.region_14.19_spmd.sunk | while | flops 2856463360 | bytes 442216320 | solution.py:262
  700.6 11.6 fusion.226
  762.9 12.8 stack.89
  775.6 20.2 %copy.488 = f32[1,62,8,64,64]{1,4,2,3,0:T(8,128)} copy(f32[1,62,8,64,64]{3,2,4,1,0:T(8,128)} %stack.89) | data formatting | bytes 16252928 | tf_op jit(solution)/shard_map/while/body/eval_jaxpr/stack | solution.py:113
  795.8 12.8 stack.88
  808.6 20.0 %copy.487 = f32[1,62,8,64,64]{1,4,2,3,0:T(8,128)} copy(f32[1,62,8,64,64]{3,2,4,1,0:T(8,128)} %stack.88) | data formatting | bytes 16252928 | tf_op jit(solution)/shard_map/while/body/eval_jaxpr/stack | solution.py:113
  873.3 17.4 %scatter-add.13 = f32[2,64,64,64]{1,3,2,0:T(8,128)} dynamic-update-slice(f32[2,64,64,64]{1,3,2,0:T(8,128)} %scatter-add.12, f32[2,1,64,64]{1,3,2,0:T(8,128)} %slice_add_fusion.5, s32[]{:T(128)} %constant.200.clone.1..sunk.1, s32[]{:T(128)} %constant.198.clone.1..sunk, s32[]{:T(128)} %constant.200.clone.1..sunk.1, s32[]{:T(128)} %constant.200.clone.1..sunk.1) | dynamic-update-slice | bytes 65540 | tf_op jit(solution)/shard_map/while/body/eval_jaxpr/scatter-add | solution.py:120
  1019.9 12.6 stack.89
  1032.5 20.0 %copy.488 = f32[1,62,8,64,64]{1,4,2,3,0:T(8,128)} copy(f32[1,62,8,64,64]{3,2,4,1,0:T(8,128)} %stack.89) | data formatting | bytes 16252928 | tf_op jit(solution)/shard_map/while/body/eval_jaxpr/stack | solution.py:113
  1052.5 12.9 stack.88
  1065.4 19.9 %copy.487 = f32[1,62,8,64,64]{1,4,2,3,0:T(8,128)} copy(f32[1,62,8,64,64]{3,2,4,1,0:T(8,128)} %stack.88) | data formatting | bytes 16252928 | tf_op jit(solution)/shard_map/while/body/eval_jaxpr/stack | solution.py:113
  1129.0 17.0 scatter-add.13
  1274.3 12.6 stack.89
  1286.9 20.0 %copy.488 = f32[1,62,8,64,64]{1,4,2,3,0:T(8,128)} copy(f32[1,62,8,64,64]{3,2,4,1,0:T(8,128)} %stack.89) | data formatting | bytes 16252928 | tf_op jit(solution)/shard_map/while/body/eval_jaxpr/stack | solution.py:113
  1306.9 12.7 stack.88
  1319.6 19.9 %copy.487 = f32[1,62,8,64,64]{1,4,2,3,0:T(8,128)} copy(f32[1,62,8,64,64]{3,2,4,1,0:T(8,128)} %stack.88) | data formatting | bytes 16252928 | tf_op jit(solution)/shard_map/while/body/eval_jaxpr/stack | solution.py:113
  1383.2 17.1 scatter-add.13
  1449.3 14.1 reshape.558
  1467.3 106.7 %all_to_all.60 = bf16[4,1024,3,1,192]{1,4,2,3,0:T(8,128)(2,1)S(1)} all-to-all(bf16[4,1024,3,1,192]{1,4,2,3,0:T(8,128)(2,1)S(1)} %copy.387), channel_id=1, replica_groups=mesh['dp'=8,'sp'=4] {'sp'}, dimensions={0} | all-to-all | bytes 9437184 | tf_op jit(solution)/shard_map/all_to_all | solution.py:269
  1609.9 39.2 %all-reduce.18 = (f32[2,768]{1,0:T(2,128)S(1)}, f32[768]{0:T(1024)S(1)}, f32[768]{0:T(1024)S(1)}, f32[768]{0:T(1024)S(1)}, f32[3072]{0:T(1024)S(1)}, /*index=5*/...) all-reduce(f32[2,768]{1,0:T(2,128)S(1)} %pad_maximum_fusion.12, ...), channel_id=3, replica_groups=mesh['dp'=8,'sp'=4] {'dp','sp'}, use_global_device_ids=true, to_apply=%region_22.23.clone | all-reduce | flops 9216 | bytes 73728
  1653.9 56.9 %reduce-scatter.14.cloned.1.call-done = f32[24,2304]{1,0:T(8,128)} async-done(((f32[768,2304]{1,0:T(8,128)}), f32[24,2304]{1,0:T(8,128)}) %reduce-scatter.14.cloned.1.call-update) | async-done | bytes 221200
  (634 shorter events, 854.5 us)
Async XLA Ops:
  7.2 71.9 %all-gather.6.cloned.1.call-start = ((), (), s32[]{:S(2)}) async-start(), calls=%async_computation.8 | async-start | bytes 3649536 | tf_op jit(solution)/shard_map/all_gather | solution.py:181
  7.9 515.2 %all-gather.8.cloned.1.call-start = ((), (), s32[]{:S(2)}) async-start(), calls=%async_computation.9 | async-start | bytes 1216512 | tf_op jit(solution)/shard_map/all_gather | solution.py:183
  8.7 518.7 %all-gather.10.cloned.1.call-start = ((), (), s32[]{:S(2)}) async-start(), calls=%async_computation.10 | async-start | bytes 4866048 | tf_op jit(solution)/shard_map/all_gather | solution.py:187
  99.4 112.7 %all-to-all-start = ((bf16[1024,3,4,192]{0,3,1,2:T(8,128)(2,1)}), bf16[1024,3,4,192]{0,3,1,2:T(8,128)(2,1)}, u32[]{:S(2)}, u32[]{:S(2)}) async-start(bf16[1024,3,4,192]{0,3,1,2:T(8,128)(2,1)} %copy.369), calls=%async_computation | async-start | bytes 9437184 | tf_op jit(solution)/shard_map/all_to_all | solution.py:207
  104.5 433.5 %all-gather.12.cloned.1.call-start = ((), (), s32[]{:S(2)}) async-start(), calls=%async_computation.11 | async-start | bytes 4866048 | tf_op jit(solution)/shard_map/all_gather | solution.py:189
  286.7 6.6 slice-start.2
  457.5 7.8 copy-start.19
  460.6 6.7 copy-start.35
  460.6 7.0 copy-start.36
  460.6 7.2 copy-start.37
  460.6 7.4 copy-start.38
  460.7 7.6 copy-start.39
  460.7 60.8 %copy-start.18 = (bf16[1,1024,768]{2,1,0:T(8,128)(2,1)S(1)}, bf16[1,1024,768]{2,1,0:T(8,128)(2,1)}, u32[]{:S(2)}) copy-start(bf16[1,1024,768]{2,1,0:T(8,128)(2,1)} %param.37) | copy-start | bytes 4718596
  460.7 62.4 %all-to-all-start.1 = ((bf16[4,1024,192]{1,2,0:T(8,128)(2,1)}), bf16[4,1024,192]{1,2,0:T(8,128)(2,1)}, u32[]{:S(2)}, u32[]{:S(2)}) async-start(bf16[4,1024,192]{1,2,0:T(8,128)(2,1)} %copy.376), calls=%async_computation.1 | async-start | bytes 3145728 | tf_op jit(solution)/shard_map/all_to_all | solution.py:217
  465.2 1188.7 %reduce-scatter.8.cloned.1.call-start = ((), (), s32[]{:S(2)}) async-start(), calls=%async_computation.12 | async-start | bytes 2433024 | tf_op jit(solution)/shard_map/reduce_scatter | solution.py:281
  549.3 6.7 slice-start.8
  552.6 21.1 %slice-start.6 = ((s8[4718592]{0:T(1024)(128)(4,1)}), s8[4194304]{0:T(1024)(128)(4,1)S(1)}, s32[]{:S(2)}) async-start(s8[4718592]{0:T(1024)(128)(4,1)} %bitcast.371), calls=%async_computation.22 | async-start | bytes 8388608
  556.0 17.7 %copy-start.21 = (bf16[1024,768]{0,1:T(8,128)(2,1)}, bf16[1024,768]{0,1:T(8,128)(2,1)S(1)}, u32[]{:S(2)}) copy-start(bf16[1024,768]{0,1:T(8,128)(2,1)S(1)} %get-tuple-element.475) | copy-start | bytes 4718596
  556.0 17.7 %slice-start.7 = ((s8[4718592]{0:T(1024)(128)(4,1)}), s8[524288]{0:T(1024)(128)(4,1)S(1)}, s32[]{:S(2)}) async-start(s8[4718592]{0:T(1024)(128)(4,1)} %bitcast.371), calls=%async_computation.23 | async-start | bytes 1048576
  590.7 1063.1 %reduce-scatter.12.cloned.1.call-start = ((), (), s32[]{:S(2)}) async-start(), calls=%async_computation.14 | async-start | bytes 9732096 | tf_op jit(solution)/shard_map/reduce_scatter | solution.py:287
  610.0 47.3 %all-to-all-start.2 = ((bf16[1024,4,192]{0,2,1:T(8,128)(2,1)}), bf16[1024,4,192]{0,2,1:T(8,128)(2,1)}, u32[]{:S(2)}, u32[]{:S(2)}) async-start(bf16[1024,4,192]{0,2,1:T(8,128)(2,1)} %bitcast.383), calls=%async_computation.2 | async-start | bytes 3145728 | tf_op jit(solution)/shard_map/all_to_all | solution.py:260
  614.4 1039.5 %reduce-scatter.10.cloned.1.call-start = ((), (), s32[]{:S(2)}) async-start(), calls=%async_computation.13 | async-start | bytes 9732096 | tf_op jit(solution)/shard_map/reduce_scatter | solution.py:285
  625.1 1085.6 %reduce-scatter.14.cloned.1.call-start = ((), (), s32[]{:S(2)}) async-start(), calls=%async_computation.15 | async-start | bytes 7299072
  700.6 14.9 copy-start.10
  731.9 9.1 copy-start.1
  731.9 11.1 slice-start
  959.6 14.9 copy-start.10
  990.0 8.0 copy-start.1
  990.0 10.1 slice-start
  1214.0 14.8 copy-start.10
  1244.4 8.0 copy-start.1
  1244.4 10.1 slice-start
  (73 other events, 275.2 us)
Sparse Core Ops, SparseCore 0:
  10.8 62.8 all-gather.5
  76.5 82.7 all-gather.7
  162.0 93.3 all-gather.9
  258.0 62.3 all-gather.11
  590.9 101.0 reduce-scatter.7
  699.3 134.4 reduce-scatter.11
  840.3 134.6 reduce-scatter.9
  1592.2 118.4 reduce-scatter.13
where the time goes:
time: 1730 us; the launch traced here: 1720 us
  local copies, waits for them, and re-layouts  729 us (42%)
  matrix products  282 us (16%)
  blocking collectives  268 us (15%)
  waiting for transfers between devices  198 us (11%)
  other arithmetic  189 us (11%)
  loops' own time  22 us (1%)
    another operation x12, local copies, waits for them, and re-layouts, head_backward(): jnp.stack([dkey_list, dvalue_list])  197 us
    all_to_all x1, waiting for transfers between devices, per_device(): lax.all_to_all(packed, 'sp', split_axis=2, concat_axis=0, tiled=True)  107 us
    all_to_all x1, blocking collectives, per_device(): lax.all_to_all(grad_heads, 'sp', split_axis=0, concat_axis=3, tiled=True)  107 us
    unnamed x2, blocking collectives  92 us
    slice x6, local copies, waits for them, and re-layouts, middle_scores(): listed[0]  77.7 us
    all_gather x1, blocking collectives, per_device(): lax.all_gather(query_value_bias, ('dp', 'sp'), axis=1, tiled=True)  69.5 us
    unnamed x9, waiting for transfers between devices  59.1 us
    while x159, local copies, waits for them, and re-layouts  59.1 us
  transfers between devices with their start and end apart: 11, of which 3 were waited for; matrix products, arithmetic and copies ran while one was open for 65% of the time, Pallas kernels for 0%

commit v1 on v0

v1 whole, which is shorter than its diff:
```python
from functools import partial

import jax
import jax.numpy as jnp
import numpy as np
from jax import lax
from jax.experimental import pallas as pl
from jax.experimental.pallas import tpu as pltpu
from jax.sharding import Mesh
from jax.sharding import PartitionSpec as P

HEAD_DIM = 64
BLOCK = 64
LANES = 128
SLOT = 4 * HEAD_DIM
EPS = 1e-05
MASKED = -1e30
ALL = ("c", "core", "zh", "zl")
GROUP = ("core", "zl")
REST = ("c", "zh")
CHUNK = 512
ROWS = 256
VMEM_BYTES = 60 * 1024 * 1024

f32 = jnp.float32
bf16 = jnp.bfloat16
NT = (((1,), (1,)), ((), ()))
TN = (((0,), (0,)), ((), ()))


def dot(a, b):
    return jnp.dot(a, b, preferred_element_type=f32)


def dot_nt(a, b):
    return lax.dot_general(a, b, NT, preferred_element_type=f32)


def dot_tn(a, b):
    return lax.dot_general(a, b, TN, preferred_element_type=f32)


def rows_at(start, size):
    return pl.ds(pl.multiple_of(start, size), size)


def listed(ref, rand_ref, head, i, blocks, randoms, cols):
    parts = [
        ref[0:BLOCK, cols],
        ref[(blocks - 1) * BLOCK : blocks * BLOCK, cols],
        ref[pl.ds(pl.multiple_of((i - 1) * BLOCK, BLOCK), 3 * BLOCK), cols],
    ]
    base = (head * (blocks - 2) + i - 1) * randoms
    for r in range(randoms):
        parts.append(ref[rows_at(rand_ref[base + r] * BLOCK, BLOCK), cols])
    return jnp.concatenate(parts, axis=0)


def mask_globals(s, i, blocks):
    lane = lax.broadcasted_iota(jnp.int32, (BLOCK, LANES), 1)
    low = lane < BLOCK
    dead = (low & (i == 1)) | (~low & (i == blocks - 2))
    return jnp.concatenate([jnp.where(dead, MASKED, s[:, :LANES]), s[:, LANES:]], axis=1)


def attend_kernel(heads, randoms, rand_ref, x_ref, w_ref, b_ref, qkv_ref, res_ref, ctx_ref):
    length = x_ref.shape[0]
    blocks = length // BLOCK
    last = (blocks - 1) * BLOCK

    def project(t, carry):
        rows = rows_at(t * CHUNK, CHUNK)
        qkv_ref[rows, :] = (dot(x_ref[rows, :], w_ref[...]) + b_ref[...]).astype(bf16)
        return carry

    lax.fori_loop(0, length // CHUNK, project, 0)

    def middle(i, carry):
        rows = rows_at(i * BLOCK, BLOCK)
        lane = lax.broadcasted_iota(jnp.int32, (BLOCK, LANES), 1)
        for h in range(heads):
            at = h * SLOT
            kv = listed(qkv_ref, rand_ref, h, i, blocks, randoms, slice(at + LANES, at + SLOT))
            s = mask_globals(dot_nt(qkv_ref[rows, at : at + LANES], kv), i, blocks)
            top = jnp.max(s, axis=1, keepdims=True)
            e = jnp.exp(s - top)
            total = jnp.sum(e, axis=1, keepdims=True)
            o = dot(e.astype(bf16), kv) / total
            res_ref[h, rows, :] = jnp.where(lane < HEAD_DIM, top + jnp.log(total), o)
        return carry

    lax.fori_loop(1, blocks - 1, middle, 0)

    for h in range(heads):
        at = h * SLOT
        q = jnp.concatenate(
            [qkv_ref[0:BLOCK, at : at + LANES], qkv_ref[last : last + BLOCK, at : at + LANES]], axis=0
        )

        def whole(t, carry, at=at, q=q):
            top, total, acc = carry
            kv = qkv_ref[rows_at(t * CHUNK, CHUNK), at + LANES : at + SLOT]
            s = dot_nt(q, kv)
            new = jnp.maximum(top, jnp.max(s, axis=1, keepdims=True))
            fade = jnp.exp(top - new)
            e = jnp.exp(s - new)
            total = total * fade + jnp.sum(e, axis=1, keepdims=True)
            return new, total, acc * fade + dot(e.astype(bf16), kv)

        top, total, acc = lax.fori_loop(
            0,
            length // CHUNK,
            whole,
            (
                jnp.full((2 * BLOCK, 1), MASKED, f32),
                jnp.zeros((2 * BLOCK, 1), f32),
                jnp.zeros((2 * BLOCK, LANES), f32),
            ),
        )
        lane = lax.broadcasted_iota(jnp.int32, (2 * BLOCK, LANES), 1)
        both = jnp.where(lane < HEAD_DIM, top + jnp.log(total), acc / total)
        res_ref[h, 0:BLOCK, :] = both[:BLOCK]
        res_ref[h, last : last + BLOCK, :] = both[BLOCK:]

    per_quarter = ctx_ref.shape[1]

    def pack(t, carry):
        part, piece = t // per_quarter, t % per_quarter
        lane = lax.broadcasted_iota(jnp.int32, (BLOCK, LANES), 1)
        low = lane < HEAD_DIM
        for n in range(ROWS // BLOCK):
            rows = rows_at(t * ROWS + n * BLOCK, BLOCK)
            first = pltpu.roll(res_ref[0, rows, :], HEAD_DIM, 1)
            pair = jnp.where(low, first, res_ref[1, rows, :])
            ctx_ref[part, piece, n * BLOCK : (n + 1) * BLOCK, :] = pair.astype(bf16)
        for n in range(ROWS // (2 * BLOCK)):
            rows = rows_at(t * ROWS + 2 * n * BLOCK, BLOCK)
            odd = rows_at(t * ROWS + (2 * n + 1) * BLOCK, BLOCK)
            first = pltpu.roll(res_ref[2, rows, :], HEAD_DIM, 1)
            both = jnp.where(low, first, res_ref[2, odd, :])
            ctx_ref[part, piece, ROWS + n * BLOCK : ROWS + (n + 1) * BLOCK, :] = both.astype(bf16)
        return carry

    lax.fori_loop(0, length // ROWS, pack, 0)


def attend(rand, x, w, b, parts, heads):
    length = x.shape[0]
    randoms = rand.size // (heads * (length // BLOCK - 2))
    vmem = pl.BlockSpec(memory_space=pltpu.VMEM)
    return pl.pallas_call(
        partial(attend_kernel, heads, randoms),
        out_shape=(
            jax.ShapeDtypeStruct((length, heads * SLOT), bf16),
            jax.ShapeDtypeStruct((heads, length, LANES), f32),
            jax.ShapeDtypeStruct((parts, length // parts // ROWS, ROWS * 3 // 2, LANES), bf16),
        ),
        in_specs=[pl.BlockSpec(memory_space=pltpu.SMEM), vmem, vmem, vmem],
        out_specs=(vmem, vmem, vmem),
        compiler_params=pltpu.CompilerParams(vmem_limit_bytes=VMEM_BYTES),
        name="attend",
    )(rand, x, w, b)


def attend_back_kernel(
    heads, randoms, rand_ref, qkv_ref, res_ref, dctx_ref, draw_ref, sums_ref, *scratch
):
    dout, acc = scratch[:heads], scratch[heads:]
    length = qkv_ref.shape[0]
    blocks = length // BLOCK
    last = (blocks - 1) * BLOCK
    per_quarter = dctx_ref.shape[1]

    def unpack(t, carry):
        part, piece = t // per_quarter, t % per_quarter
        lane = lax.broadcasted_iota(jnp.int32, (BLOCK, LANES), 1)
        low = lane < HEAD_DIM
        for n in range(ROWS // BLOCK):
            rows = rows_at(t * ROWS + n * BLOCK, BLOCK)
            pair = dctx_ref[part, piece, n * BLOCK : (n + 1) * BLOCK, :].astype(f32)
            dout[0][rows, :] = jnp.where(low, 0.0, pltpu.roll(pair, HEAD_DIM, 1)).astype(bf16)
            dout[1][rows, :] = jnp.where(low, 0.0, pair).astype(bf16)
        for n in range(ROWS // (2 * BLOCK)):
            rows = rows_at(t * ROWS + 2 * n * BLOCK, BLOCK)
            odd = rows_at(t * ROWS + (2 * n + 1) * BLOCK, BLOCK)
            both = dctx_ref[part, piece, ROWS + n * BLOCK : ROWS + (n + 1) * BLOCK, :].astype(f32)
            dout[2][rows, :] = jnp.where(low, 0.0, pltpu.roll(both, HEAD_DIM, 1)).astype(bf16)
            dout[2][odd, :] = jnp.where(low, 0.0, both).astype(bf16)
        return carry

    lax.fori_loop(0, length // ROWS, unpack, 0)

    step = 256
    for h in range(heads):
        at = h * SLOT
        q = jnp.concatenate(
            [qkv_ref[0:BLOCK, at : at + LANES], qkv_ref[last : last + BLOCK, at : at + LANES]], axis=0
        )
        g = jnp.concatenate([dout[h][0:BLOCK, :], dout[h][last : last + BLOCK, :]], axis=0)
        res = jnp.concatenate([res_ref[h, 0:BLOCK, :], res_ref[h, last : last + BLOCK, :]], axis=0)
        log_total = res[:, 0:1]
        delta = jnp.sum(g.astype(f32) * res, axis=1, keepdims=True)
        both = jnp.concatenate([q, g], axis=0)

        def whole(t, dq, at=at, h=h, both=both, log_total=log_total, delta=delta):
            rows = rows_at(t * step, step)
            kv = qkv_ref[rows, at + LANES : at + SLOT]
            sd = dot_nt(both, kv)
            p = jnp.exp(sd[: 2 * BLOCK] - log_total)
            ds = (p * (sd[2 * BLOCK :] - delta)).astype(bf16)
            acc[h][rows, :] = dot_tn(jnp.concatenate([ds, p.astype(bf16)], axis=0), both)
            return dq + dot(ds, kv)

        dq = lax.fori_loop(0, length // step, whole, jnp.zeros((2 * BLOCK, LANES), f32))
        lane = lax.broadcasted_iota(jnp.int32, (2 * BLOCK, LANES), 1)
        dq = jnp.where(lane < HEAD_DIM, dq, 0.0).astype(bf16)
        draw_ref[0:BLOCK, at : at + LANES] = dq[:BLOCK]
        draw_ref[last : last + BLOCK, at : at + LANES] = dq[BLOCK:]

    def middle(i, carry):
        rows = rows_at(i * BLOCK, BLOCK)
        lane = lax.broadcasted_iota(jnp.int32, (BLOCK, LANES), 1)
        for h in range(heads):
            at = h * SLOT
            kv = listed(qkv_ref, rand_ref, h, i, blocks, randoms, slice(at + LANES, at + SLOT))
            g = dout[h][rows, :]
            res = res_ref[h, rows, :]
            both = jnp.concatenate([qkv_ref[rows, at : at + LANES], g], axis=0)
            delta = jnp.sum(g.astype(f32) * res, axis=1, keepdims=True)
            sd = dot_nt(both, kv)
            p = jnp.exp(mask_globals(sd[:BLOCK], i, blocks) - res[:, 0:1])
            ds = (p * (sd[BLOCK:] - delta)).astype(bf16)
            dkv = dot_tn(jnp.concatenate([ds, p.astype(bf16)], axis=0), both)
            dq = dot(ds, kv)
            draw_ref[rows, at : at + LANES] = jnp.where(lane < HEAD_DIM, dq, 0.0).astype(bf16)
            acc[h][0:BLOCK, :] += dkv[0:BLOCK]
            acc[h][last : last + BLOCK, :] += dkv[BLOCK : 2 * BLOCK]
            near = pl.ds(pl.multiple_of((i - 1) * BLOCK, BLOCK), 3 * BLOCK)
            acc[h][near, :] += dkv[2 * BLOCK : 5 * BLOCK]
            base = (h * (blocks - 2) + i - 1) * randoms
            for r in range(randoms):
                far = rows_at(rand_ref[base + r] * BLOCK, BLOCK)
                acc[h][far, :] += dkv[(5 + r) * BLOCK : (6 + r) * BLOCK]
        return carry

    lax.fori_loop(1, blocks - 1, middle, 0)
    sums_ref[...] = jnp.zeros_like(sums_ref)

    def finish(t, carry):
        rows = rows_at(t * CHUNK, CHUNK)
        for h in range(heads):
            at = h * SLOT
            draw_ref[rows, at + LANES : at + SLOT] = acc[h][rows, :].astype(bf16)
        sums_ref[0:1, :] += jnp.sum(draw_ref[rows, :].astype(f32), axis=0, keepdims=True)
        return carry

    lax.fori_loop(0, length // CHUNK, finish, 0)


def attend_back(rand, qkv, res, dctx, heads):
    length = qkv.shape[0]
    randoms = rand.size // (heads * (length // BLOCK - 2))
    vmem = pl.BlockSpec(memory_space=pltpu.VMEM)
    return pl.pallas_call(
        partial(attend_back_kernel, heads, randoms),
        out_shape=(
            jax.ShapeDtypeStruct((length, heads * SLOT), bf16),
            jax.ShapeDtypeStruct((8, heads * SLOT), f32),
        ),
        in_specs=[pl.BlockSpec(memory_space=pltpu.SMEM), vmem, vmem, vmem],
        out_specs=(vmem, vmem),
        scratch_shapes=[pltpu.VMEM((length, LANES), bf16)] * heads
        + [pltpu.VMEM((length, LANES), f32)] * heads,
        compiler_params=pltpu.CompilerParams(vmem_limit_bytes=VMEM_BYTES),
        name="attend_back",
    )(rand, qkv, res, dctx)


def mean_of(a):
    return jnp.mean(a, axis=1, keepdims=True)


def norm(r):
    center = r - mean_of(r)
    rstd = lax.rsqrt(mean_of(center * center) + EPS)
    return center * rstd, rstd


def norm_back(dn, n, rstd):
    return rstd * (dn - mean_of(dn) - n * mean_of(dn * n))


def rowsum(a):
    return jnp.sum(a, axis=0, keepdims=True)


def chain_kernel(
    groups,
    ctx_ref,
    tok_ref,
    og_ref,
    wo_ref,
    wu_ref,
    wd_ref,
    vec_ref,
    bu_ref,
    out_ref,
    dres_ref,
    dctx_ref,
    mix_ref,
    hid_ref,
    act_ref,
    dpre_ref,
    dffn_ref,
    dproj_ref,
    gvec_ref,
    gbu_ref,
    slope_ref,
    wop_ref,
):
    width = tok_ref.shape[1]
    hidden = wu_ref.shape[1]
    wide = 3 * HEAD_DIM
    step = pl.program_id(0)

    @pl.when(step == 0)
    def _():
        for g in range(groups):
            wop_ref[g * LANES : (g + 1) * LANES, :] = wo_ref[g * wide : g * wide + LANES, :]
            to = groups * LANES + g * HEAD_DIM
            wop_ref[to : to + HEAD_DIM, :] = wo_ref[g * wide + LANES : (g + 1) * wide, :]
        gvec_ref[...] = jnp.zeros_like(gvec_ref)
        gbu_ref[...] = jnp.zeros_like(gbu_ref)

    low = lax.broadcasted_iota(jnp.int32, (BLOCK, LANES), 1) < HEAD_DIM
    for g in range(groups):
        mix_ref[:, g * LANES : (g + 1) * LANES] = ctx_ref[g, 0, :ROWS, :]
    for g in range(0, groups, 2):
        to = groups * LANES + g * HEAD_DIM
        for n in range(ROWS // (2 * BLOCK)):
            at = ROWS + n * BLOCK
            a = ctx_ref[g, 0, at : at + BLOCK, :].astype(f32)
            b = ctx_ref[g + 1, 0, at : at + BLOCK, :].astype(f32)
            even = jnp.where(low, a, pltpu.roll(b, HEAD_DIM, 1))
            odd = jnp.where(low, pltpu.roll(a, HEAD_DIM, 1), b)
            r = 2 * n * BLOCK
            mix_ref[r : r + BLOCK, to : to + LANES] = even.astype(bf16)
            mix_ref[r + BLOCK : r + 2 * BLOCK, to : to + LANES] = odd.astype(bf16)

    bo, g1, s1 = vec_ref[0:1, :], vec_ref[1:2, :], vec_ref[2:3, :]
    bd, g2, s2 = vec_ref[3:4, :], vec_ref[4:5, :], vec_ref[5:6, :]
    n1, rstd1 = norm(tok_ref[...].astype(f32) + dot(mix_ref[...], wop_ref[...]) + bo)
    hid = n1 * g1 + s1
    hid_low = hid.astype(bf16)
    hid_ref[...] = hid_low
    scale = np.sqrt(2.0 / np.pi).astype(np.float32)

    def up(f, carry):
        cols = rows_at(f * CHUNK, CHUNK)
        u = dot(hid_low, wu_ref[:, cols]) + bu_ref[:, cols]
        square = u * u
        t = jnp.tanh(scale * (u + 0.044715 * (u * square)))
        half = 0.5 * (1.0 + t)
        act_ref[:, cols] = (u * half).astype(bf16)
        slope = half + 0.5 * u * (1.0 - t * t) * (scale * (1.0 + (3 * 0.044715) * square))
        slope_ref[:, cols] = slope.astype(bf16)
        return carry

    lax.fori_loop(0, hidden // CHUNK, up, 0)
    n2, rstd2 = norm(hid + dot(act_ref[...], wd_ref[...]) + bd)
    out_ref[...] = (n2 * g2 + s2).astype(bf16)
    og = og_ref[...].astype(f32)
    gvec_ref[4:5, :] += rowsum(og * n2)
    gvec_ref[5:6, :] += rowsum(og)
    dres2 = norm_back(og * g2, n2, rstd2)
    dffn = dres2.astype(bf16)
    dffn_ref[...] = dffn
    gvec_ref[3:4, :] += rowsum(dffn.astype(f32))

    def down_back(f, carry):
        cols = rows_at(f * CHUNK, CHUNK)
        dact = dot_nt(dffn, wd_ref[cols, :])
        dpre = (dact * slope_ref[:, cols].astype(f32)).astype(bf16)
        dpre_ref[:, cols] = dpre
        gbu_ref[0:1, cols] += rowsum(dpre.astype(f32))
        return carry

    lax.fori_loop(0, hidden // CHUNK, down_back, 0)
    dh = dres2 + dot_nt(dpre_ref[...], wu_ref[...])
    gvec_ref[1:2, :] += rowsum(dh * n1)
    gvec_ref[2:3, :] += rowsum(dh)
    dres1 = norm_back(dh * g1, n1, rstd1)
    dres_ref[...] = dres1
    dproj = dres1.astype(bf16)
    dproj_ref[...] = dproj
    gvec_ref[0:1, :] += rowsum(dproj.astype(f32))
    dmix = dot_nt(dproj, wop_ref[...])
    for g in range(groups):
        dctx_ref[g, 0, :ROWS, :] = dmix[:, g * LANES : (g + 1) * LANES].astype(bf16)
    for g in range(0, groups, 2):
        to = groups * LANES + g * HEAD_DIM
        for n in range(ROWS // (2 * BLOCK)):
            at = ROWS + n * BLOCK
            r = 2 * n * BLOCK
            even = dmix[r : r + BLOCK, to : to + LANES]
            odd = dmix[r + BLOCK : r + 2 * BLOCK, to : to + LANES]
            a = jnp.where(low, even, pltpu.roll(odd, HEAD_DIM, 1))
            b = jnp.where(low, pltpu.roll(even, HEAD_DIM, 1), odd)
            dctx_ref[g, 0, at : at + BLOCK, :] = a.astype(bf16)
            dctx_ref[g + 1, 0, at : at + BLOCK, :] = b.astype(bf16)


def chain(ctx, tok, og, wo, wu, wd, vec, bu):
    rows, width = tok.shape
    hidden = wu.shape[1]
    groups = ctx.shape[0]
    once = pl.Buffered(1)

    def tiled(cols):
        return pl.BlockSpec((ROWS, cols), lambda t: (t, 0))

    def fixed(shape):
        return pl.BlockSpec(shape, lambda t: (0, 0), pipeline_mode=once)

    packed = pl.BlockSpec((groups, 1) + ctx.shape[2:], lambda t: (0, t, 0, 0))
    shape = jax.ShapeDtypeStruct
    return pl.pallas_call(
        partial(chain_kernel, groups),
        grid=(rows // ROWS,),
        out_shape=(
            shape((rows, width), bf16),
            shape((rows, width), f32),
            shape(ctx.shape, bf16),
            shape((rows, width), bf16),
            shape((rows, width), bf16),
            shape((rows, hidden), bf16),
            shape((rows, hidden), bf16),
            shape((rows, width), bf16),
            shape((rows, width), bf16),
            shape((8, width), f32),
            shape((8, hidden), f32),
        ),
        in_specs=[
            packed,
            tiled(width),
            tiled(width),
            fixed(wo.shape),
            fixed(wu.shape),
            fixed(wd.shape),
            fixed(vec.shape),
            fixed(bu.shape),
        ],
        out_specs=(
            tiled(width),
            tiled(width),
            packed,
            tiled(width),
            tiled(width),
            tiled(hidden),
            tiled(hidden),
            tiled(width),
            tiled(width),
            pl.BlockSpec((8, width), lambda t: (0, 0)),
            pl.BlockSpec((8, hidden), lambda t: (0, 0)),
        ),
        scratch_shapes=[pltpu.VMEM((ROWS, hidden), bf16), pltpu.VMEM(wo.shape, bf16)],
        compiler_params=pltpu.CompilerParams(vmem_limit_bytes=VMEM_BYTES),
        name="chain",
    )(ctx, tok, og, wo, wu, wd, vec, bu)


def per_device(
    tokens,
    qkv_weight,
    query_value_bias,
    out_weight,
    out_bias,
    norm1_gain,
    norm1_bias,
    up_weight,
    up_bias,
    down_weight,
    down_bias,
    norm2_gain,
    norm2_bias,
    rand_blocks,
    out_grad,
):
    members = lax.axis_size(GROUP)
    devices = lax.axis_size(ALL)
    swap = [(0, 0), (1, 2), (2, 1), (3, 3)]

    def move(a):
        return lax.ppermute(a, ("core", "zh"), swap)

    tok = move(tokens[0])
    og = move(out_grad[0])
    rand = move(rand_blocks[0])
    heads = rand.shape[0]
    rows, width = tok.shape
    cols = heads * HEAD_DIM
    group = lax.axis_index(GROUP)

    x = lax.all_gather(tok, GROUP, axis=0, tiled=True)
    w_qkv = lax.all_gather(qkv_weight, ALL, axis=0, tiled=True)
    w_out = lax.all_gather(out_weight, ALL, axis=0, tiled=True)
    w_up = lax.all_gather(up_weight, ALL, axis=0, tiled=True)
    w_down = lax.all_gather(down_weight, ALL, axis=0, tiled=True)
    own = width // devices
    small = jnp.concatenate(
        [
            query_value_bias[0],
            query_value_bias[1],
            out_bias,
            norm1_gain,
            norm1_bias,
            down_bias,
            norm2_gain,
            norm2_bias,
            up_bias,
        ]
    )
    small = lax.all_gather(small, ALL, axis=0).astype(f32)
    vecs = jnp.transpose(small[:, : 8 * own].reshape(devices, 8, own), (1, 0, 2)).reshape(8, width)
    bias_up = small[:, 8 * own :].reshape(1, -1)

    def lay_out(a):
        a = a.reshape(a.shape[:-2] + (3, heads, HEAD_DIM))
        q, k, v = a[..., 0, :, :], a[..., 1, :, :], a[..., 2, :, :]
        q = q * jnp.asarray(HEAD_DIM**-0.5, a.dtype)
        laid = jnp.stack([q, jnp.zeros_like(q), k, v], axis=-2)
        return laid.reshape(laid.shape[:-3] + (heads * SLOT,))

    w_own = lax.dynamic_slice_in_dim(
        w_qkv.reshape(width, 3, members, cols), group, 1, axis=2
    ).reshape(width, 3, cols)
    w_own = lay_out(w_own)
    bias3 = jnp.stack([vecs[0], jnp.zeros_like(vecs[0]), vecs[1]]).reshape(3, members, cols)
    b_own = lay_out(lax.dynamic_slice_in_dim(bias3, group, 1, axis=1).reshape(1, 3, cols))
    rand_flat = rand.reshape(-1)

    qkv, res, ctx_send = attend(rand_flat, x, w_own, b_own, members, heads)
    ctx = lax.all_to_all(ctx_send, GROUP, split_axis=0, concat_axis=0, tiled=True)
    chain_vecs = jnp.concatenate([vecs[2:8], jnp.zeros((2, width), f32)], axis=0)
    out, dres1, dctx_send, mix, hid, act, dpre, dffn, dproj, gvec, gbu = chain(
        ctx, tok, og, w_out, w_up, w_down, chain_vecs, bias_up
    )
    dctx = lax.all_to_all(dctx_send, GROUP, split_axis=0, concat_axis=0, tiled=True)
    out = move(out)

    g_down = dot_tn(act, dffn).astype(bf16)
    g_up = dot_tn(hid, dpre).astype(bf16)
    g_mix = dot_tn(mix, dproj).astype(bf16)
    pairs = g_mix[: members * LANES].reshape(members, LANES, width)
    thirds = g_mix[members * LANES :].reshape(members, HEAD_DIM, width)
    g_out = jnp.concatenate([pairs, thirds], axis=1).reshape(width, width)

    def scatter(a):
        return lax.psum_scatter(a, ALL, scatter_dimension=0, tiled=True).astype(f32)

    g_down, g_up, g_out = scatter(g_down), scatter(g_up), scatter(g_out)

    draw, sums = attend_back(rand_flat, qkv, res, dctx, heads)
    dx = dot_nt(draw, w_own).astype(bf16)
    dx = lax.psum_scatter(dx, GROUP, scatter_dimension=0, tiled=True)
    input_grad = move((dres1 + dx.astype(f32)).astype(bf16)).astype(f32)

    def strip(a):
        a = a.reshape(a.shape[:-1] + (heads, 4, HEAD_DIM))
        q, k, v = a[..., 0, :] * (HEAD_DIM**-0.5), a[..., 2, :], a[..., 3, :]
        return jnp.stack([q, k, v], axis=-3).reshape(a.shape[:-3] + (3, cols))

    g_qkv = strip(dot_tn(x, draw)).reshape(-1, 2, 2, members // 2, own, 3 * cols)
    g_qkv = jnp.transpose(g_qkv, (0, 2, 1, 3, 4, 5)).reshape(-1, members, own, 3 * cols)
    g_qkv = g_qkv.reshape(-1, 3 * cols).astype(bf16)
    g_qkv = lax.psum_scatter(g_qkv, REST, scatter_dimension=0, tiled=True)
    g_qkv = g_qkv.reshape(members, own, 3 * cols)
    g_qkv = lax.all_to_all(g_qkv, GROUP, split_axis=0, concat_axis=0, tiled=True).astype(f32)
    g_qkv = jnp.transpose(g_qkv.reshape(members, own, 3, cols), (1, 2, 0, 3)).reshape(own, -1)

    col_sums = strip(sums[0:1])[0]
    pair = jnp.stack([col_sums[0], col_sums[2]]).reshape(2, 1, cols)
    mine = (jnp.arange(members) == group)[None, :, None]
    pair = jnp.where(mine, pair, 0.0).reshape(2, width)
    vec_grads = jnp.concatenate([pair, gvec[0:6]], axis=0).reshape(8, devices, own)
    vec_grads = jnp.transpose(vec_grads, (1, 0, 2)).reshape(devices, 8 * own)
    vec_grads = jnp.concatenate([vec_grads, gbu[0].reshape(devices, -1)], axis=1)
    vec_grads = lax.psum_scatter(vec_grads, ALL, scatter_dimension=0, tiled=True)[0]
    v8 = vec_grads[: 8 * own].reshape(8, own)
    return (
        out[None],
        input_grad[None],
        g_qkv,
        v8[0:2],
        g_out,
        v8[2],
        v8[3],
        v8[4],
        g_up,
        vec_grads[8 * own :],
        g_down,
        v8[5],
        v8[6],
        v8[7],
    )


def solution(mesh):
    dp, sp = mesh.shape["dp"], mesh.shape["sp"]
    fine = Mesh(mesh.devices.reshape(dp // 2, 2, 2, sp // 2), ALL)
    dp, sp = ("c", "core"), ("zh", "zl")
    act = P(dp, sp, None)
    mat = P(ALL, None)
    pair = P(None, ALL)
    vec = P(ALL)
    rand = P(dp, sp, None, None)
    return jax.shard_map(
        per_device,
        mesh=fine,
        in_specs=(act, mat, pair, mat, vec, vec, vec, mat, vec, mat, vec, vec, vec, rand, act),
        out_specs=(act, act, mat, pair, mat, vec, vec, vec, mat, vec, mat, vec, vec, vec),
        check_vma=False,
    )
```

time: 1730 us -> 1110 us (0.64)
  local copies, waits for them, and re-layouts: 729 us -> 30.4 us
  waiting for transfers between devices: 198 us -> 586 us
  matrix products: 282 us -> 40.1 us
  Pallas kernels: 0 us -> 233 us
  other arithmetic: 189 us -> 11.4 us
  blocking collectives: 268 us -> 153 us
  starting transfers between devices: 14.6 us -> 39.4 us
  loops' own time: 22 us -> 0 us
    reduce_scatter x3 -> x5, waiting for transfers between devices: 0.01 us -> 387 us  [the longest x3 309 us: scatter(): return lax.psum_scatter(a, ALL, scatter_dimension=0, tiled=True).astype(f32)]
    dot_general x57 -> x5, matrix products: 282 us -> 40.1 us  [the longest x4 30.4 us: dot_tn(): return lax.dot_general(a, b, TN, preferred_element_type=f32)]
    pallas_call x0 -> x3, Pallas kernels: none -> 233 us  [the longest x1 95.6 us: attend_back(): pl.pallas_call(partial(attend_back_kernel, heads, randoms), out_shape=(ja...]
    another operation x20 -> x10, local copies, waits for them, and re-layouts: 213 us -> 2.26 us  [the longest x2 1.64 us: strip(): return jnp.stack([q, k, v], axis=-3).reshape(a.shape[:-3] + (3, cols))]
    all_gather x4 -> x5, waiting for transfers between devices: 0.04 us -> 194 us  [the longest x1 85 us: per_device(): x = lax.all_gather(tok, GROUP, axis=0, tiled=True)]
    all_to_all x3 -> x2, waiting for transfers between devices: 139 us -> 2.64 us  [the longest x1 2.64 us: per_device(): lax.all_to_all(g_qkv, GROUP, split_axis=0, concat_axis=0, tiled=True)]
    slice x24 -> x14, local copies, waits for them, and re-layouts: 115 us -> 4.16 us  [the longest x1 0.93 us: per_device(): gbu[0].reshape(devices, -1)]
    scatter-add x6 -> x0, local copies, waits for them, and re-layouts: 85.6 us -> none  [the longest x3 51.4 us: head_backward(): pair_total.at[:, blocks - 1].add(jnp.sum(slot_grads[:, :, 4], axis=1))]
  transfers between devices with their start and end apart: 11 -> 17, of which waited for: 3 -> 9; matrix products, arithmetic and copies ran while one was open for 65% -> 6% of each run, Pallas kernels for 0% -> 7%
where the time goes in v1:
time: 1110 us
  waiting for transfers between devices  586 us (53%)
  Pallas kernels  233 us (21%)
  blocking collectives  153 us (14%)
  matrix products  40.1 us (4%)
  starting transfers between devices  39.4 us (4%)
  local copies, waits for them, and re-layouts  30.4 us (3%)
  between operations  14.6 us (1%)
  other arithmetic  11.4 us (1%)
    reduce_scatter x3, waiting for transfers between devices, scatter(): return lax.psum_scatter(a, ALL, scatter_dimension=0, tiled=True).astype(f32)  309 us
    unnamed x2, blocking collectives  128 us
    pallas_call x1, Pallas kernels, attend_back(): pl.pallas_call(partial(attend_back_kernel, heads, randoms), out_shape=(ja...  95.6 us
    all_gather x1, waiting for transfers between devices, per_device(): x = lax.all_gather(tok, GROUP, axis=0, tiled=True)  85 us
    pallas_call x1, Pallas kernels, attend(): pl.pallas_call(partial(attend_kernel, heads, randoms), out_shape=(jax.Sha...  82.1 us
    reduce_scatter x1, waiting for transfers between devices, per_device(): dx = lax.psum_scatter(dx, GROUP, scatter_dimension=0, tiled=True)  72.5 us
    all_gather x1, waiting for transfers between devices, per_device(): w_down = lax.all_gather(down_weight, ALL, axis=0, tiled=True)  67.1 us
    pallas_call x1, Pallas kernels, chain(): pl.pallas_call(partial(chain_kernel, groups), grid=(rows // ROWS,), out_s...  55.4 us
  transfers between devices with their start and end apart: 17, of which 9 were waited for; matrix products, arithmetic and copies ran while one was open for 6% of the time, Pallas kernels for 7%

profile of v1, /device:TPU:0, one launch (start us, length us, event | category | flops | bytes accessed | tf_op | source)
XLA Modules:
  0.0 1108.3 jit_solution(9002796645314877328)
XLA Ops:
  8.1 2.1 collective-permute-start.1
  14.5 87.8 %all-reduce.1 = bf16[9216]{0:T(1024)(128)(2,1)S(1)} all-reduce(bf16[9216]{0:T(1024)(128)(2,1)S(1)} %dynamic-update-slice), channel_id=2, replica_groups=mesh['c'=4,'core'=2,'zh'=2,'zl'=2] {'c','core','zh','zl'}, use_global_device_ids=true, to_apply=%add.1 | all-reduce | flops 9216 | bytes 36864
  105.3 4.5 copy.66
  111.7 85.0 %all-gather.7.cloned.1.call-done.x_ref = bf16[4096,768]{1,0:T(8,128)(2,1)} async-done(((bf16[1024,768]{1,0:T(8,128)(2,1)}), bf16[4096,768]{1,0:T(8,128)(2,1)}) %all-gather.7.cloned.1.call-update) | async-done | bytes 6291472 | tf_op jit(solution)/shard_map/all_gather | solution.py:504
  196.7 82.1 %attend.1 = (bf16[4096,768]{1,0:T(8,128)(2,1)}, f32[3,4096,128]{2,1,0:T(8,128)}, bf16[4,4,384,128]{3,2,1,0:T(8,128)(2,1)}) custom-call(s32[558]{0:T(1024)} %reshape.184.rand_ref, bf16[4096,768]{1,0:T(8,128)(2,1)} %all-gather.7.cloned.1.call-done.x_ref, bf16[768,768]{1,0:T(8,128)(2,1)} %copy.71.w_ref, f32[1,768]{1,0:T(1,128)} %reshape.188.b_ref), custom_call_target="tpu_custom_call" | custom-call | tf_op jit(solution)/shard_map/attend/pallas_call | solution.py:151
  278.7 3.7 all-to-all-start
  282.5 13.4 %collective-permute-start.2 = (bf16[1024,768]{1,0:T(8,128)(2,1)}, bf16[1024,768]{1,0:T(8,128)(2,1)}, u32[]{:S(2)}, u32[]{:S(2)}) collective-permute-start(bf16[1024,768]{1,0:T(8,128)(2,1)} %bitcast.99), channel_id=1, source_target_pairs={{0,0},{2,4},{4,2},{6,6},{1,1},{3,5},{5,3},{7,7},{8,8},{10,12},{12,... | collective-permute-start | bytes 4718600 | tf_op jit(solution)/shard_map/ppermute | solution.py:494
  298.2 41.7 %all-gather.13.cloned.1.call-done.wu_ref = bf16[768,3072]{1,0:T(8,128)(2,1)} async-done(((bf16[24,3072]{1,0:T(8,128)(2,1)}), bf16[768,3072]{1,0:T(8,128)(2,1)}) %all-gather.13.cloned.1.call-update) | async-done | bytes 4718608 | tf_op jit(solution)/shard_map/all_gather | solution.py:507
  339.9 67.1 %all-gather.15.cloned.1.call-done.wd_ref = bf16[3072,768]{1,0:T(8,128)(2,1)} async-done(((bf16[96,768]{1,0:T(8,128)(2,1)}), bf16[3072,768]{1,0:T(8,128)(2,1)}) %all-gather.15.cloned.1.call-update) | async-done | bytes 4718608 | tf_op jit(solution)/shard_map/all_gather | solution.py:508
  408.1 55.4 %chain.1 = (bf16[1024,768]{1,0:T(8,128)(2,1)}, f32[1024,768]{1,0:T(8,128)}, bf16[4,4,384,128]{3,2,1,0:T(8,128)(2,1)}, bf16[1024,768]{1,0:T(8,128)(2,1)}, bf16[10...) custom-call(bf16[4,4,384,128]{3,2,1,0:T(8,128)(2,1)} %copy-done.1, ...), custom_call_target="tpu_custom_call" | custom-call | tf_op jit(solution)/shard_map/chain/pallas_call | solution.py:427
  463.5 24.7 %all_to_all.15.dctx_ref = bf16[4,4,384,128]{3,2,1,0:T(8,128)(2,1)} all-to-all(bf16[4,4,384,128]{3,2,1,0:T(8,128)(2,1)} %get-tuple-element.35), channel_id=1, replica_groups=mesh['c'=4,'core'=2,'zh'=2,'zl'=2] {'core','zl'}, dimensions={0} | all-to-all | bytes 3145728 | tf_op jit(solution)/shard_map/all_to_all | solution.py:548
  488.2 95.6 %attend_back.1 = (bf16[4096,768]{1,0:T(8,128)(2,1)}, f32[8,768]{1,0:T(8,128)}) custom-call(s32[558]{0:T(1024)} %reshape.184.rand_ref, bf16[4096,768]{1,0:T(8,128)(2,1)} %get-tuple-element.33.qkv_ref, f32[3,4096,128]{2,1,0:T(8,128)} %get-tuple-element.34.res_ref, bf16[4,4,384,128]{3,2,1,0:T(8,128)(2,1)} %all_to_all.15.dctx_ref), custom_call_target="tpu_custom_call" | custom-call | tf_op jit(solution)/shard_map/attend_back/pallas_call | solution.py:264
  583.8 9.7 convolution_convert_fusion
  598.2 9.7 fusion.8
  609.7 1.7 convert_element_type.46
  613.1 9.7 convolution_convert_fusion.1
  624.2 9.5 convolution_convert_fusion.2
  633.8 13.6 %collective-permute-start.3 = (bf16[1024,768]{1,0:T(8,128)(2,1)}, bf16[1024,768]{1,0:T(8,128)(2,1)}, u32[]{:S(2)}, u32[]{:S(2)}) collective-permute-start(bf16[1024,768]{1,0:T(8,128)(2,1)} %get-tuple-element.31), channel_id=1, source_target_pairs={{0,0},{2,4},{4,2},{6,6},{1,1},{3,5},{5,3},{7,7},{8,8},{10,12},{12,... | collective-permute-start | bytes 4718600 | tf_op jit(solution)/shard_map/ppermute | solution.py:494
  647.4 72.5 %reduce-scatter.6.cloned.1.call-done = bf16[1024,768]{1,0:T(8,128)(2,1)} async-done(((bf16[4096,768]{1,0:T(8,128)(2,1)}), bf16[1024,768]{1,0:T(8,128)(2,1)}) %reduce-scatter.6.cloned.1.call-update) | async-done | bytes 1572880 | tf_op jit(solution)/shard_map/reduce_scatter | solution.py:565
  719.9 2.9 add_convert_fusion
  722.8 2.1 collective-permute-start.4
  726.2 95.1 %reduce-scatter.10.cloned.1.call-done = bf16[24,768]{1,0:T(8,128)(2,1)} async-done(((bf16[768,768]{1,0:T(8,128)(2,1)}), bf16[24,768]{1,0:T(8,128)(2,1)}) %reduce-scatter.10.cloned.1.call-update) | async-done | bytes 36880 | tf_op jit(solution)/shard_map/reduce_scatter | solution.py:559
  824.2 40.5 %all-reduce.2 = f32[32,288]{1,0:T(8,128)S(1)} all-reduce(f32[32,288]{1,0:T(8,128)S(1)} %pad_maximum_fusion.3), channel_id=5, replica_groups=mesh['c'=4,'core'=2,'zh'=2,'zl'=2] {'c','core','zh','zl'}, use_global_device_ids=true, to_apply=%region_2.0.clone | all-reduce | flops 9216 | bytes 73728
  864.6 6.3 reduce-scatter.8.cloned.1.call-done
  870.9 3.3 all-to-all-start.2
  876.1 2.6 all-to-all-done.2
  880.1 103.8 %reduce-scatter.14.cloned.1.call-done = bf16[96,768]{1,0:T(8,128)(2,1)} async-done(((bf16[3072,768]{1,0:T(8,128)(2,1)}), bf16[96,768]{1,0:T(8,128)(2,1)}) %reduce-scatter.14.cloned.1.call-update) | async-done | bytes 147472 | tf_op jit(solution)/shard_map/reduce_scatter | solution.py:559
  983.9 1.6 convert_element_type.54
  985.5 109.7 %reduce-scatter.12.cloned.1.call-done = bf16[24,3072]{1,0:T(8,128)(2,1)} async-done(((bf16[768,3072]{1,0:T(8,128)(2,1)}), bf16[24,3072]{1,0:T(8,128)(2,1)}) %reduce-scatter.12.cloned.1.call-update) | async-done | bytes 147472 | tf_op jit(solution)/shard_map/reduce_scatter | solution.py:559
  1095.2 1.6 convert_element_type.52
  1096.9 1.9 bitcast_convert_fusion
  1098.8 2.7 copy.90
  (137 shorter events, 30.1 us)
Async XLA Ops:
  7.2 6.0 copy-start.7
  7.2 6.8 copy-start.8
  7.2 6.8 copy-start.9
  7.2 6.8 copy-start.10
  7.2 6.8 copy-start.11
  7.2 6.8 copy-start.15
  7.2 6.8 copy-start.12
  7.3 6.8 copy-start.13
  7.3 6.8 copy-start.14
  7.3 98.0 %all-gather.9.cloned.1.call-start = ((), (), s32[]{:S(2)}) async-start(), calls=%async_computation.9 | async-start | bytes 3649536 | tf_op jit(solution)/shard_map/all_gather | solution.py:505
  8.0 188.7 %all-gather.7.cloned.1.call-start = ((), (), s32[]{:S(2)}) async-start(), calls=%async_computation.8 | async-start | bytes 7864320 | tf_op jit(solution)/shard_map/all_gather | solution.py:504
  8.1 2.1 collective-permute-start.1
  11.3 286.9 %all-gather.11.cloned.1.call-start = ((), (), s32[]{:S(2)}) async-start(), calls=%async_computation.10 | async-start | bytes 1216512 | tf_op jit(solution)/shard_map/all_gather | solution.py:506
  12.0 327.8 %all-gather.13.cloned.1.call-start = ((), (), s32[]{:S(2)}) async-start(), calls=%async_computation.11 | async-start | bytes 4866048 | tf_op jit(solution)/shard_map/all_gather | solution.py:507
  12.6 394.4 %all-gather.15.cloned.1.call-start = ((), (), s32[]{:S(2)}) async-start(), calls=%async_computation.12 | async-start | bytes 4866048 | tf_op jit(solution)/shard_map/all_gather | solution.py:508
  13.2 91.1 %collective-permute-start = (s32[3,62,3]{1,2,0:T(4,128)S(1)}, s32[3,62,3]{1,2,0:T(4,128)S(1)}, u32[]{:S(2)}, u32[]{:S(2)}) collective-permute-start(s32[3,62,3]{1,2,0:T(4,128)S(1)} %bitcast.97), channel_id=1, source_target_pairs={{0,0},{2,4},{4,2},{6,6},{1,1},{3,5},{5,3},{7,7},{8,8},{10,12},{12,... | collective-permute-start | bytes 6704 | tf_op jit(solution)/shard_map/ppermute | solution.py:494
  103.1 2.2 copy-start.3
  278.7 17.1 %copy-start.4 = (f32[32,8,24]{2,1,0:T(8,128)S(1)}, f32[32,8,24]{2,1,0:T(8,128)}, u32[]{:S(2)}) copy-start(f32[32,8,24]{2,1,0:T(8,128)} %copy-done.3) | copy-start | bytes 73732
  278.7 128.2 %all-to-all-start = ((bf16[4,4,384,128]{3,2,1,0:T(8,128)(2,1)}), bf16[4,4,384,128]{3,2,1,0:T(8,128)(2,1)S(1)}, u32[]{:S(2)}, u32[]{:S(2)}) async-start(bf16[4,4,384,128]{3,2,1,0:T(8,128)(2,1)} %get-tuple-element.30), calls=%async_computation | async-start | bytes 3145728 | tf_op jit(solution)/shard_map/all_to_all | solution.py:543
  282.5 437.5 %reduce-scatter.6.cloned.1.call-start = ((), (), s32[]{:S(2)}) async-start(), calls=%async_computation.13 | async-start | bytes 7864320 | tf_op jit(solution)/shard_map/reduce_scatter | solution.py:565
  282.5 15.7 %collective-permute-start.2 = (bf16[1024,768]{1,0:T(8,128)(2,1)}, bf16[1024,768]{1,0:T(8,128)(2,1)}, u32[]{:S(2)}, u32[]{:S(2)}) collective-permute-start(bf16[1024,768]{1,0:T(8,128)(2,1)} %bitcast.99), channel_id=1, source_target_pairs={{0,0},{2,4},{4,2},{6,6},{1,1},{3,5},{5,3},{7,7},{8,8},{10,12},{12,... | collective-permute-start | bytes 4718600 | tf_op jit(solution)/shard_map/ppermute | solution.py:494
  593.5 1.9 copy-start.19
  593.6 227.7 %reduce-scatter.10.cloned.1.call-start = ((), (), s32[]{:S(2)}) async-start(), calls=%async_computation.15 | async-start | bytes 1216512 | tf_op jit(solution)/shard_map/reduce_scatter | solution.py:559
  598.1 272.8 %reduce-scatter.8.cloned.1.call-start = ((), (), s32[]{:S(2)}) async-start(), calls=%async_computation.14 | async-start | bytes 1105920 | tf_op jit(solution)/shard_map/reduce_scatter | solution.py:576
  611.4 1.8 copy-start.17
  612.5 371.4 %reduce-scatter.14.cloned.1.call-start = ((), (), s32[]{:S(2)}) async-start(), calls=%async_computation.17 | async-start | bytes 4866048 | tf_op jit(solution)/shard_map/reduce_scatter | solution.py:559
  622.9 472.4 %reduce-scatter.12.cloned.1.call-start = ((), (), s32[]{:S(2)}) async-start(), calls=%async_computation.16 | async-start | bytes 4866048 | tf_op jit(solution)/shard_map/reduce_scatter | solution.py:559
  633.7 86.2 %copy-start.2 = (f32[1024,768]{1,0:T(8,128)S(1)}, f32[1024,768]{1,0:T(8,128)}, u32[]{:S(2)}) copy-start(f32[1024,768]{1,0:T(8,128)} %get-tuple-element.32) | copy-start | bytes 9437188
  633.8 92.4 %collective-permute-start.3 = (bf16[1024,768]{1,0:T(8,128)(2,1)}, bf16[1024,768]{1,0:T(8,128)(2,1)}, u32[]{:S(2)}, u32[]{:S(2)}) collective-permute-start(bf16[1024,768]{1,0:T(8,128)(2,1)} %get-tuple-element.31), channel_id=1, source_target_pairs={{0,0},{2,4},{4,2},{6,6},{1,1},{3,5},{5,3},{7,7},{8,8},{10,12},{12,... | collective-permute-start | bytes 4718600 | tf_op jit(solution)/shard_map/ppermute | solution.py:494
  719.9 5.1 copy-start.6
  722.8 374.1 %collective-permute-start.4 = (bf16[1024,768]{1,0:T(8,128)(2,1)}, bf16[1024,768]{1,0:T(8,128)(2,1)S(1)}, u32[]{:S(2)}, u32[]{:S(2)}) collective-permute-start(bf16[1024,768]{1,0:T(8,128)(2,1)} %add_convert_fusion), channel_id=1, source_target_pairs={{0,0},{2,4},{4,2},{6,6},{1,1},{3,5},{5,3},{7,7},{8,8},{10,12},{12,... | collective-permute-start | bytes 4718600 | tf_op jit(solution)/shard_map/ppermute | solution.py:494
  870.9 7.8 all-to-all-start.2
  (5 other events, 5.7 us)
Sparse Core Ops, SparseCore 0:
  10.9 72.2 all-gather.8
  85.4 111.2 all-gather.6
  199.5 54.3 all-gather.10
  256.6 83.2 all-gather.12
  342.5 64.4 all-gather.14
  593.7 126.2 reduce-scatter.5
  725.0 96.1 reduce-scatter.9
  824.9 45.9 reduce-scatter.7
  877.3 106.5 reduce-scatter.13
  989.2 105.9 reduce-scatter.11

commit v2 on v1

--- a/solution.py
+++ b/solution.py
@@ -469,6 +469,246 @@
     )(ctx, tok, og, wo, wu, wd, vec, bu)
 
 
+MESH = pl.DeviceIdType.MESH
+
+
+def run_phases(items):
+    step = 0
+    live = list(items)
+    while live:
+        after = []
+        for first, phases in live:
+            if first > step or next(phases, None) is not None:
+                after.append((first, phases))
+        live = after
+        step += 1
+
+
+class Where:
+    def __init__(self):
+        c, core, zh, zl = (lax.axis_index(a) for a in ALL)
+        self.y, self.x, self.core, self.zh, self.zl = c // 2, c % 2, core, zh, zl
+        self.z = zh * 2 + zl
+        self.by_x = (self.y * 2 + 1 - self.x, core, zh, zl)
+        self.by_y = ((1 - self.y) * 2 + self.x, core, zh, zl)
+        self.by_core = (c, 1 - core, zh, zl)
+        self.by_zl = (c, core, zh, 1 - zl)
+        self.by_zh = (c, core, 1 - zh, zl)
+        self.by_mid = (c, core, 1 - zh, 1 - zl)
+        self.by_swap = (c, 1 - core, 1 - zh, zl)
+        self.inner = zh != zl
+        self.stays = core == zh
+
+    def greet(self):
+        barrier = pltpu.get_barrier_semaphore()
+        others = (self.by_x, self.by_y, self.by_core, self.by_zl, self.by_zh, self.by_mid, self.by_swap)
+        for other in others:
+            pl.semaphore_signal(barrier, inc=1, device_id=other, device_id_type=MESH)
+        pl.semaphore_wait(barrier, len(others))
+
+
+class Copies:
+    def __init__(self, send, recv, local):
+        self.send, self.recv, self.local_sems = send, recv, local
+        self.n = self.m = 0
+
+    def remote(self, src, dst, device):
+        n = self.n
+        self.n += 1
+        return pltpu.make_async_remote_copy(
+            src_ref=src,
+            dst_ref=dst,
+            send_sem=self.send.at[n],
+            recv_sem=self.recv.at[n],
+            device_id=device,
+            device_id_type=MESH,
+        )
+
+    def local(self, src, dst):
+        m = self.m
+        self.m += 1
+        return pltpu.make_async_copy(src, dst, self.local_sems.at[m])
+
+
+def gather_item(me, copies, shard, full, cols, x_first):
+    y, x, core, zh, zl = me.y, me.x, me.core, me.zh, me.zl
+    mine = shard.at[:, cols]
+    own = copies.local(mine, full.at[y, x, core, me.z, :, cols])
+    first = copies.remote(mine, full.at[y, x, core, me.z, :, cols], me.by_zl)
+    own.start()
+    first.start()
+    yield 1
+    own.wait()
+    first.wait()
+    pair = full.at[y, x, core, pl.ds(zh * 2, 2), :, cols]
+    pair_far = full.at[y, x, core, pl.ds((1 - zh) * 2, 2), :, cols]
+    middle = copies.remote(pair, pair, me.by_mid)
+    onward = copies.remote(pair_far, pair_far, me.by_zl)
+
+    @pl.when(me.inner)
+    def _():
+        middle.start()
+
+    yield 1
+
+    @pl.when(me.inner)
+    def _():
+        middle.wait()
+        onward.start()
+
+    yield 1
+
+    @pl.when(me.inner)
+    def _():
+        onward.wait_send()
+
+    @pl.when(jnp.logical_not(me.inner))
+    def _():
+        onward.wait_recv()
+
+    line = full.at[y, x, core, :, :, cols]
+    near = copies.remote(line, line, me.by_x if x_first else me.by_y)
+    near.start()
+    across = [copies.remote(line, line, me.by_core)]
+    across[0].start()
+    yield 1
+    near.wait()
+    if x_first:
+        block = full.at[y, :, core, :, :, cols]
+        got = full.at[y, 1 - x, core, :, :, cols]
+        rest = full.at[1 - y, :, core, :, :, cols]
+    else:
+        block = full.at[:, x, core, :, :, cols]
+        got = full.at[1 - y, x, core, :, :, cols]
+        rest = full.at[:, 1 - x, core, :, :, cols]
+    far = copies.remote(block, block, me.by_y if x_first else me.by_x)
+    far.start()
+    across.append(copies.remote(got, got, me.by_core))
+    across[1].start()
+    yield 1
+    far.wait()
+    across.append(copies.remote(rest, rest, me.by_core))
+    across[2].start()
+    yield 1
+    for copy in across:
+        copy.wait()
+
+
+def tokens_item(me, copies, tok, x_all, piece):
+    place = me.core * 2 + me.zl
+    there = (1 - me.core) * 2 + me.zl
+    out = copies.remote(tok.at[piece], x_all.at[there, piece], me.by_swap)
+    keep = copies.local(tok.at[piece], x_all.at[place, piece])
+
+    @pl.when(me.stays)
+    def _():
+        keep.start()
+
+    @pl.when(jnp.logical_not(me.stays))
+    def _():
+        out.start()
+
+    yield 1
+
+    @pl.when(me.stays)
+    def _():
+        keep.wait()
+
+    @pl.when(jnp.logical_not(me.stays))
+    def _():
+        out.wait()
+
+    held = x_all.at[place, piece]
+    along = copies.remote(held, held, me.by_zl)
+    along.start()
+    over = copies.remote(held, held, me.by_core)
+    over.start()
+    yield 1
+    along.wait()
+    came = x_all.at[me.core * 2 + 1 - me.zl, piece]
+    onto = copies.remote(came, came, me.by_core)
+    onto.start()
+    yield 1
+    over.wait()
+    onto.wait()
+
+
+def exchange_item(me, copies, src, dst):
+    out = copies.remote(src, dst, me.by_swap)
+    keep = copies.local(src, dst)
+
+    @pl.when(me.stays)
+    def _():
+        keep.start()
+
+    @pl.when(jnp.logical_not(me.stays))
+    def _():
+        out.start()
+
+    yield 1
+
+    @pl.when(me.stays)
+    def _():
+        keep.wait()
+
+    @pl.when(jnp.logical_not(me.stays))
+    def _():
+        out.wait()
+
+
+PIECES = 4
+
+
+def gather_kernel(
+    tok, og, qkv, w_out, up, down, small, x_all, og_all, qkv_all, out_all, up_all, down_all, small_all, *sems
+):
+    me = Where()
+    me.greet()
+    copies = Copies(*sems)
+    items = []
+
+    def halves(first, shard, full):
+        half = shard.shape[1] // 2
+        for n in range(2):
+            items.append((first, gather_item(me, copies, shard, full, slice(n * half, (n + 1) * half), n == 0)))
+
+    items.append((0, gather_item(me, copies, small, small_all, slice(0, LANES), True)))
+    for piece in range(PIECES):
+        items.append((piece, tokens_item(me, copies, tok, x_all, piece)))
+        if piece == 0:
+            halves(0, qkv, qkv_all)
+    halves(1, w_out, out_all)
+    halves(2, up, up_all)
+    halves(3, down, down_all)
+    items.append((4, exchange_item(me, copies, og, og_all)))
+    items.sort(key=lambda item: item[0])
+    run_phases(items)
+
+
+def gather(tok, og, mats, small, members):
+    rows, width = tok.shape
+    hbm = pl.BlockSpec(memory_space=pltpu.HBM)
+    shape = jax.ShapeDtypeStruct
+    tok = tok.reshape(PIECES, rows // PIECES, width)
+    outs = [shape((members,) + tok.shape, bf16), shape(og.shape, bf16)]
+    outs += [shape((2, 2, 2, 4) + a.shape, bf16) for a in (*mats, small)]
+    return pl.pallas_call(
+        gather_kernel,
+        out_shape=tuple(outs),
+        in_specs=[hbm] * 7,
+        out_specs=(hbm,) * 7,
+        scratch_shapes=[
+            pltpu.SemaphoreType.DMA((112,)),
+            pltpu.SemaphoreType.DMA((112,)),
+            pltpu.SemaphoreType.DMA((16,)),
+        ],
+        compiler_params=pltpu.CompilerParams(
+            collective_id=0, has_side_effects=True, vmem_limit_bytes=VMEM_BYTES
+        ),
+        name="gather",
+    )(tok, og, *mats, small)
+
+
 def per_device(
     tokens,
     qkv_weight,
@@ -493,19 +733,11 @@
     def move(a):
         return lax.ppermute(a, ("core", "zh"), swap)
 
-    tok = move(tokens[0])
-    og = move(out_grad[0])
     rand = move(rand_blocks[0])
     heads = rand.shape[0]
-    rows, width = tok.shape
+    rows, width = tokens.shape[1:]
     cols = heads * HEAD_DIM
     group = lax.axis_index(GROUP)
-
-    x = lax.all_gather(tok, GROUP, axis=0, tiled=True)
-    w_qkv = lax.all_gather(qkv_weight, ALL, axis=0, tiled=True)
-    w_out = lax.all_gather(out_weight, ALL, axis=0, tiled=True)
-    w_up = lax.all_gather(up_weight, ALL, axis=0, tiled=True)
-    w_down = lax.all_gather(down_weight, ALL, axis=0, tiled=True)
     own = width // devices
     small = jnp.concatenate(
         [
@@ -520,7 +752,22 @@
             up_bias,
         ]
     )
-    small = lax.all_gather(small, ALL, axis=0).astype(f32)
+    mats = (qkv_weight, out_weight, up_weight, down_weight)
+    direct = lax.axis_size("c") == 4 and members == 4 and own % 8 == 0
+    if direct:
+        count = small.shape[0]
+        padded = jnp.pad(small, (0, 16 * LANES - count)).reshape(16, LANES)
+        x, og, *full, small = gather(tokens[0], out_grad[0], mats, padded, members)
+        x = x.reshape(members * rows, width)
+        tok = lax.dynamic_slice_in_dim(x, group * rows, rows, axis=0)
+        w_qkv, w_out, w_up, w_down = (a.reshape(-1, a.shape[-1]) for a in full)
+        small = small.reshape(devices, -1)[:, :count].astype(f32)
+    else:
+        tok = move(tokens[0])
+        og = move(out_grad[0])
+        x = lax.all_gather(tok, GROUP, axis=0, tiled=True)
+        w_qkv, w_out, w_up, w_down = (lax.all_gather(a, ALL, axis=0, tiled=True) for a in mats)
+        small = lax.all_gather(small, ALL, axis=0).astype(f32)
     vecs = jnp.transpose(small[:, : 8 * own].reshape(devices, 8, own), (1, 0, 2)).reshape(8, width)
     bias_up = small[:, 8 * own :].reshape(1, -1)
 

time: 1110 us -> 998 us (0.90)
  waiting for transfers between devices: 586 us -> 396 us
  Pallas kernels: 233 us -> 388 us
  blocking collectives: 153 us -> 64.9 us
  local copies, waits for them, and re-layouts: 30.4 us -> 58.8 us
  starting transfers between devices: 39.4 us -> 23.7 us
    all_gather x5 -> x0, waiting for transfers between devices: 194 us -> none  [the longest x1 85 us: per_device(): x = lax.all_gather(tok, GROUP, axis=0, tiled=True)]
    pallas_call x0 -> x1, Pallas kernels: none -> 155 us  [gather(): pl.pallas_call(gather_kernel, out_shape=tuple(outs), in_specs=[hbm] * 7,...]
    unnamed x2 -> x1, blocking collectives: 128 us -> 40.4 us
    all_to_all x1, waiting for transfers between devices: 0.01 us -> 15.6 us  [per_device(): lax.all_to_all(ctx_send, GROUP, split_axis=0, concat_axis=0, tiled=True)]
    ppermute x5 -> x3, starting transfers between devices: 31.8 us -> 16.2 us  [move(): return lax.ppermute(a, ('core', 'zh'), swap)]
  transfers between devices with their start and end apart: 17 -> 10, of which waited for: 9 -> 7; matrix products, arithmetic and copies ran while one was open for 6% -> 9% of each run, Pallas kernels for 7% -> 16%
where the time goes in v2:
time: 998 us; the launch traced here: 996 us
  waiting for transfers between devices  396 us (40%)
  Pallas kernels  388 us (39%)
  blocking collectives  64.9 us (7%)
  local copies, waits for them, and re-layouts  58.8 us (6%)
  matrix products  39.7 us (4%)
  starting transfers between devices  23.7 us (2%)
  between operations  14.1 us (1%)
  other arithmetic  11.3 us (1%)
    reduce_scatter x3, waiting for transfers between devices, scatter(): return lax.psum_scatter(a, ALL, scatter_dimension=0, tiled=True).astype(f32)  309 us
    pallas_call x1, Pallas kernels, gather(): pl.pallas_call(gather_kernel, out_shape=tuple(outs), in_specs=[hbm] * 7,...  155 us
    pallas_call x1, Pallas kernels, attend_back(): pl.pallas_call(partial(attend_back_kernel, heads, randoms), out_shape=(ja...  95.6 us
    pallas_call x1, Pallas kernels, attend(): pl.pallas_call(partial(attend_kernel, heads, randoms), out_shape=(jax.Sha...  82.1 us
    reduce_scatter x1, waiting for transfers between devices, per_device(): dx = lax.psum_scatter(dx, GROUP, scatter_dimension=0, tiled=True)  62.4 us
    pallas_call x1, Pallas kernels, chain(): pl.pallas_call(partial(chain_kernel, groups), grid=(rows // ROWS,), out_s...  55.4 us
    unnamed x1, blocking collectives  40.4 us
    dot_general x4, matrix products, dot_tn(): return lax.dot_general(a, b, TN, preferred_element_type=f32)  30 us
  transfers between devices with their start and end apart: 10, of which 7 were waited for; matrix products, arithmetic and copies ran while one was open for 9% of the time, Pallas kernels for 16%

profile of v2, /device:TPU:0, one launch (start us, length us, event | category | flops | bytes accessed | tf_op | source)
XLA Modules:
  0.0 995.8 jit_solution(3107622707988482622)
XLA Ops:
  9.4 4.8 concatenate.19
  14.8 154.5 %gather.1 = (bf16[4,4,256,768]{3,2,1,0:T(8,128)(2,1)}, bf16[1024,768]{1,0:T(8,128)(2,1)}, bf16[2,2,2,4,24,2304]{5,4,3,2,1,0:T(8,128)(2,1)}, bf16[2,2,2,4,24,768]...) custom-call(bf16[4,256,768]{2,1,0:T(8,128)(2,1)} %bitcast.120, ...), custom_call_target="tpu_custom_call" | custom-call | tf_op jit(solution)/shard_map/gather/pallas_call | solution.py:695
  170.8 9.9 reshape_reshape.11
  180.7 4.8 constant_dynamic-slice_fusion.1
  185.5 2.1 copy.69
  191.1 82.1 %attend.1 = (bf16[4096,768]{1,0:T(8,128)(2,1)}, f32[3,4096,128]{2,1,0:T(8,128)}, bf16[4,4,384,128]{3,2,1,0:T(8,128)(2,1)}) custom-call(s32[558]{0:T(1024)} %reshape.198.rand_ref, bf16[4096,768]{1,0:T(8,128)(2,1)} %bitcast.106, bf16[768,768]{1,0:T(8,128)(2,1)} %copy.74.w_ref, f32[1,768]{1,0:T(1,128)} %reshape.204.b_ref), custom_call_target="tpu_custom_call" | custom-call | tf_op jit(solution)/shard_map/attend/pallas_call | solution.py:151
  273.2 3.6 all-to-all-start
  278.5 2.6 constant_dynamic-slice_fusion.tok_ref
  281.2 15.6 %all-to-all-done.ctx_ref = bf16[4,4,384,128]{3,2,1,0:T(8,128)(2,1)S(1)} async-done(((bf16[4,4,384,128]{3,2,1,0:T(8,128)(2,1)}), bf16[4,4,384,128]{3,2,1,0:T(8,128)(2,1)S(1)}, u32[]{:S(2)}, u32[]{:S(2)}) %all-to-all-start) | async-done | bytes 1572896 | tf_op jit(solution)/shard_map/all_to_all | solution.py:790
  297.9 55.4 %chain.1 = (bf16[1024,768]{1,0:T(8,128)(2,1)}, f32[1024,768]{1,0:T(8,128)}, bf16[4,4,384,128]{3,2,1,0:T(8,128)(2,1)}, bf16[1024,768]{1,0:T(8,128)(2,1)}, bf16[10...) custom-call(bf16[4,4,384,128]{3,2,1,0:T(8,128)(2,1)} %copy-done, ...), custom_call_target="tpu_custom_call" | custom-call | tf_op jit(solution)/shard_map/chain/pallas_call | solution.py:427
  353.3 24.5 %all_to_all.15.dctx_ref = bf16[4,4,384,128]{3,2,1,0:T(8,128)(2,1)} all-to-all(bf16[4,4,384,128]{3,2,1,0:T(8,128)(2,1)} %get-tuple-element.49), channel_id=1, replica_groups=mesh['c'=4,'core'=2,'zh'=2,'zl'=2] {'core','zl'}, dimensions={0} | all-to-all | bytes 3145728 | tf_op jit(solution)/shard_map/all_to_all | solution.py:795
  377.8 95.6 %attend_back.1 = (bf16[4096,768]{1,0:T(8,128)(2,1)}, f32[8,768]{1,0:T(8,128)}) custom-call(s32[558]{0:T(1024)} %reshape.198.rand_ref, bf16[4096,768]{1,0:T(8,128)(2,1)} %get-tuple-element.47.qkv_ref, f32[3,4096,128]{2,1,0:T(8,128)} %get-tuple-element.48.res_ref, bf16[4,4,384,128]{3,2,1,0:T(8,128)(2,1)} %all_to_all.15.dctx_ref), custom_call_target="tpu_custom_call" | custom-call | tf_op jit(solution)/shard_map/attend_back/pallas_call | solution.py:264
  473.4 9.7 convolution_convert_fusion
  487.9 8.7 copy.76
  496.7 9.3 fusion.9
  507.7 1.7 convert_element_type.48
  511.2 9.8 convolution_convert_fusion.1
  522.3 9.5 convolution_convert_fusion.2
  531.9 13.5 %collective-permute-start.1 = (bf16[1024,768]{1,0:T(8,128)(2,1)}, bf16[1024,768]{1,0:T(8,128)(2,1)}, u32[]{:S(2)}, u32[]{:S(2)}) collective-permute-start(bf16[1024,768]{1,0:T(8,128)(2,1)} %get-tuple-element.45), channel_id=1, source_target_pairs={{0,0},{2,4},{4,2},{6,6},{1,1},{3,5},{5,3},{7,7},{8,8},{10,12},{12,... | collective-permute-start | bytes 4718600 | tf_op jit(solution)/shard_map/ppermute | solution.py:734
  545.4 62.4 %reduce-scatter.6.cloned.1.call-done = bf16[1024,768]{1,0:T(8,128)(2,1)} async-done(((bf16[4096,768]{1,0:T(8,128)(2,1)}), bf16[1024,768]{1,0:T(8,128)(2,1)}) %reduce-scatter.6.cloned.1.call-update) | async-done | bytes 1572880 | tf_op jit(solution)/shard_map/reduce_scatter | solution.py:812
  607.8 2.9 add_convert_fusion
  610.7 2.1 collective-permute-start.2
  614.0 95.1 %reduce-scatter.10.cloned.1.call-done = bf16[24,768]{1,0:T(8,128)(2,1)} async-done(((bf16[768,768]{1,0:T(8,128)(2,1)}), bf16[24,768]{1,0:T(8,128)(2,1)}) %reduce-scatter.10.cloned.1.call-update) | async-done | bytes 36880 | tf_op jit(solution)/shard_map/reduce_scatter | solution.py:806
  712.1 40.4 %all-reduce.2 = f32[32,288]{1,0:T(8,128)S(1)} all-reduce(f32[32,288]{1,0:T(8,128)S(1)} %pad_maximum_fusion.3), channel_id=4, replica_groups=mesh['c'=4,'core'=2,'zh'=2,'zl'=2] {'c','core','zh','zl'}, use_global_device_ids=true, to_apply=%region_2.3.clone | all-reduce | flops 9216 | bytes 73728
  752.5 6.4 reduce-scatter.8.cloned.1.call-done
  758.9 3.3 all-to-all-start.2
  764.1 2.6 all-to-all-done.2
  768.0 103.6 %reduce-scatter.14.cloned.1.call-done = bf16[96,768]{1,0:T(8,128)(2,1)} async-done(((bf16[3072,768]{1,0:T(8,128)(2,1)}), bf16[96,768]{1,0:T(8,128)(2,1)}) %reduce-scatter.14.cloned.1.call-update) | async-done | bytes 147472 | tf_op jit(solution)/shard_map/reduce_scatter | solution.py:806
  873.3 109.8 %reduce-scatter.12.cloned.1.call-done = bf16[24,3072]{1,0:T(8,128)(2,1)} async-done(((bf16[768,3072]{1,0:T(8,128)(2,1)}), bf16[24,3072]{1,0:T(8,128)(2,1)}) %reduce-scatter.12.cloned.1.call-update) | async-done | bytes 147472 | tf_op jit(solution)/shard_map/reduce_scatter | solution.py:806
  983.1 1.6 convert_element_type.54
  984.7 1.9 bitcast_convert_fusion
  986.6 2.7 copy.93
  (95 shorter events, 29.3 us)
Async XLA Ops:
  7.9 182.3 %collective-permute-start = (s32[3,62,3]{1,2,0:T(4,128)S(1)}, s32[3,62,3]{1,2,0:T(4,128)S(1)}, u32[]{:S(2)}, u32[]{:S(2)}) collective-permute-start(s32[3,62,3]{1,2,0:T(4,128)S(1)} %bitcast.131), channel_id=1, source_target_pairs={{0,0},{2,4},{4,2},{6,6},{1,1},{3,5},{5,3},{7,7},{8,8},{10,12},{12,... | collective-permute-start | bytes 6704 | tf_op jit(solution)/shard_map/ppermute | solution.py:734
  273.2 23.6 %all-to-all-start = ((bf16[4,4,384,128]{3,2,1,0:T(8,128)(2,1)}), bf16[4,4,384,128]{3,2,1,0:T(8,128)(2,1)S(1)}, u32[]{:S(2)}, u32[]{:S(2)}) async-start(bf16[4,4,384,128]{3,2,1,0:T(8,128)(2,1)} %get-tuple-element.40), calls=%async_computation | async-start | bytes 3145728 | tf_op jit(solution)/shard_map/all_to_all | solution.py:790
  276.8 331.1 %reduce-scatter.6.cloned.1.call-start = ((), (), s32[]{:S(2)}) async-start(), calls=%async_computation.8 | async-start | bytes 7864320 | tf_op jit(solution)/shard_map/reduce_scatter | solution.py:812
  296.8 1.1 copy-start
  483.1 1.4 copy-start.5
  483.1 1.9 copy-start.6
  483.1 226.0 %reduce-scatter.10.cloned.1.call-start = ((), (), s32[]{:S(2)}) async-start(), calls=%async_computation.10 | async-start | bytes 1216512 | tf_op jit(solution)/shard_map/reduce_scatter | solution.py:806
  487.7 271.2 %reduce-scatter.8.cloned.1.call-start = ((), (), s32[]{:S(2)}) async-start(), calls=%async_computation.9 | async-start | bytes 1105920 | tf_op jit(solution)/shard_map/reduce_scatter | solution.py:823
  509.4 1.8 copy-start.4
  510.5 361.1 %reduce-scatter.14.cloned.1.call-start = ((), (), s32[]{:S(2)}) async-start(), calls=%async_computation.12 | async-start | bytes 4866048 | tf_op jit(solution)/shard_map/reduce_scatter | solution.py:806
  520.9 1.4 copy-start.3
  521.0 462.1 %reduce-scatter.12.cloned.1.call-start = ((), (), s32[]{:S(2)}) async-start(), calls=%async_computation.11 | async-start | bytes 4866048 | tf_op jit(solution)/shard_map/reduce_scatter | solution.py:806
  531.9 76.0 %copy-start.1 = (f32[1024,768]{1,0:T(8,128)S(1)}, f32[1024,768]{1,0:T(8,128)}, u32[]{:S(2)}) copy-start(f32[1024,768]{1,0:T(8,128)} %get-tuple-element.46) | copy-start | bytes 9437188
  531.9 82.2 %collective-permute-start.1 = (bf16[1024,768]{1,0:T(8,128)(2,1)}, bf16[1024,768]{1,0:T(8,128)(2,1)}, u32[]{:S(2)}, u32[]{:S(2)}) collective-permute-start(bf16[1024,768]{1,0:T(8,128)(2,1)} %get-tuple-element.45), channel_id=1, source_target_pairs={{0,0},{2,4},{4,2},{6,6},{1,1},{3,5},{5,3},{7,7},{8,8},{10,12},{12,... | collective-permute-start | bytes 4718600 | tf_op jit(solution)/shard_map/ppermute | solution.py:734
  607.8 5.1 copy-start.2
  610.7 374.0 %collective-permute-start.2 = (bf16[1024,768]{1,0:T(8,128)(2,1)}, bf16[1024,768]{1,0:T(8,128)(2,1)S(1)}, u32[]{:S(2)}, u32[]{:S(2)}) collective-permute-start(bf16[1024,768]{1,0:T(8,128)(2,1)} %add_convert_fusion), channel_id=1, source_target_pairs={{0,0},{2,4},{4,2},{6,6},{1,1},{3,5},{5,3},{7,7},{8,8},{10,12},{12,... | collective-permute-start | bytes 4718600 | tf_op jit(solution)/shard_map/ppermute | solution.py:734
  758.9 7.8 all-to-all-start.2
Sparse Core Ops, SparseCore 0:
  483.3 124.5 reduce-scatter.5
  612.9 96.2 reduce-scatter.9
  712.8 46.0 reduce-scatter.7
  765.1 106.5 reduce-scatter.13
  877.0 106.0 reduce-scatter.11

commit v3 on v2

--- a/solution.py
+++ b/solution.py
@@ -496,12 +496,14 @@
         self.by_zh = (c, core, 1 - zh, zl)
         self.by_mid = (c, core, 1 - zh, 1 - zl)
         self.by_swap = (c, 1 - core, 1 - zh, zl)
+        self.by_both = (c, 1 - core, zh, 1 - zl)
         self.inner = zh != zl
         self.stays = core == zh
 
     def greet(self):
         barrier = pltpu.get_barrier_semaphore()
-        others = (self.by_x, self.by_y, self.by_core, self.by_zl, self.by_zh, self.by_mid, self.by_swap)
+        others = (self.by_x, self.by_y, self.by_core, self.by_zl)
+        others += (self.by_zh, self.by_mid, self.by_swap, self.by_both)
         for other in others:
             pl.semaphore_signal(barrier, inc=1, device_id=other, device_id_type=MESH)
         pl.semaphore_wait(barrier, len(others))
@@ -707,6 +709,227 @@
         ),
         name="gather",
     )(tok, og, *mats, small)
+
+
+def add_rows(dst, a, b, rows):
+    step = next(n for n in (48, 32, 24, 16, 8) if rows % n == 0)
+
+    def body(t, carry):
+        at = rows_at(t * step, step)
+        dst[at, :] = (a[at, :].astype(f32) + b[at, :].astype(f32)).astype(dst.dtype)
+        return carry
+
+    lax.fori_loop(0, rows // step, body, 0)
+
+
+def scatter_item(me, copies, src, cols, acc, from_core, from_first, from_second, from_zh, part, from_zl, out, x_first):
+    y, x, core, zh, zl = me.y, me.x, me.core, me.zh, me.zl
+    rows = acc.shape[2]
+    own = copies.local(src.at[:, :, core, :, cols], acc)
+    over = copies.remote(src.at[:, :, 1 - core, :, cols], from_core, me.by_core)
+    own.start()
+    over.start()
+    yield 1
+    own.wait()
+    over.wait()
+    for a in range(2):
+        for b in range(2):
+            add_rows(acc.at[a, b], acc.at[a, b], from_core.at[a, b], rows)
+    if x_first:
+        first = copies.remote(acc.at[:, 1 - x], from_first, me.by_x)
+    else:
+        first = copies.remote(acc.at[1 - y], from_first, me.by_y)
+    first.start()
+    yield 1
+    first.wait()
+    for a in range(2):
+        block = acc.at[a, x] if x_first else acc.at[y, a]
+        add_rows(block, block, from_first.at[a], rows)
+    if x_first:
+        second = copies.remote(acc.at[1 - y, x], from_second, me.by_y)
+    else:
+        second = copies.remote(acc.at[y, 1 - x], from_second, me.by_x)
+    second.start()
+    yield 1
+    second.wait()
+    block = acc.at[y, x]
+    add_rows(block, block, from_second, rows)
+    half = rows // 2
+    third = copies.remote(block.at[rows_at((1 - zh) * half, half)], from_zh, me.by_zh)
+    third.start()
+    yield 1
+    third.wait()
+    add_rows(part, block.at[rows_at(zh * half, half)], from_zh, half)
+    last = half // 2
+    fourth = copies.remote(part.at[rows_at((1 - zl) * last, last)], from_zl, me.by_zl)
+    fourth.start()
+    yield 1
+    fourth.wait()
+    add_rows(out, part.at[rows_at(zl * last, last)], from_zl, last)
+
+
+def scatter_buffers(rows, cols, kind):
+    return [
+        pltpu.VMEM((2, 2, rows, cols), kind),
+        pltpu.VMEM((2, 2, rows, cols), kind),
+        pltpu.VMEM((2, rows, cols), kind),
+        pltpu.VMEM((rows, cols), kind),
+        pltpu.VMEM((rows // 2, cols), kind),
+        pltpu.VMEM((rows // 2, cols), f32),
+        pltpu.VMEM((rows // 4, cols), f32),
+    ]
+
+
+def own_columns_item(me, copies, src, acc, from_x, from_y, from_zh, part, out):
+    y, x, core, zh, zl = me.y, me.x, me.core, me.zh, me.zl
+    rows = src.shape[4]
+    keep = copies.local(src.at[:, x], acc)
+    first = copies.remote(src.at[:, 1 - x], from_x, me.by_x)
+    keep.start()
+    first.start()
+    yield 1
+    keep.wait()
+    first.wait()
+    for a in range(2):
+        for b in range(2):
+            for c in range(2):
+                add_rows(acc.at[a, b, c], acc.at[a, b, c], from_x.at[a, b, c], rows)
+    second = copies.remote(acc.at[1 - y], from_y, me.by_y)
+    second.start()
+    yield 1
+    second.wait()
+    for b in range(2):
+        for c in range(2):
+            block = acc.at[y, b, c]
+            add_rows(block, block, from_y.at[b, c], rows)
+    third = copies.remote(acc.at[y, :, 1 - zh], from_zh, me.by_zh)
+    third.start()
+    yield 1
+    third.wait()
+    half = rows // 2
+    for b in range(2):
+        add_rows(part.at[b], acc.at[y, b, zh], from_zh.at[b], rows)
+    place = core * 2 + zl
+    mine = rows_at(zl * half, half)
+    other = rows_at((1 - zl) * half, half)
+    keep = copies.local(part.at[core, mine], out.at[place])
+    keep.start()
+    moves = [
+        copies.remote(part.at[core, other], out.at[place], me.by_zl),
+        copies.remote(part.at[1 - core, mine], out.at[place], me.by_core),
+        copies.remote(part.at[1 - core, other], out.at[place], me.by_both),
+    ]
+    for move in moves:
+        move.start()
+    yield 1
+    keep.wait()
+    for move in moves:
+        move.wait()
+
+
+def input_grad_item(me, copies, dx, dres, piece, acc, from_core, from_zl, res, send, out):
+    core, zl = me.core, me.zl
+    rows = acc.shape[1]
+    keep = copies.local(dx.at[core, :, piece], acc)
+    more = copies.local(dres.at[piece], res)
+    over = copies.remote(dx.at[1 - core, :, piece], from_core, me.by_core)
+    keep.start()
+    more.start()
+    over.start()
+    yield 1
+    keep.wait()
+    over.wait()
+    add_rows(acc.at[1 - zl], acc.at[1 - zl], from_core.at[1 - zl], rows)
+    along = copies.remote(acc.at[1 - zl], from_zl, me.by_zl)
+    along.start()
+    add_rows(acc.at[zl], acc.at[zl], from_core.at[zl], rows)
+    more.wait()
+    add_rows(res, res, acc.at[zl], rows)
+    yield 1
+    along.wait()
+    add_rows(send, res, from_zl, rows)
+    yield from exchange_item(me, copies, send, out.at[piece])
+
+
+SPLITS = ((0, 2), (1, 4), (2, 1), (3, 1))
+
+
+def scatter_kernel(*refs):
+    down, up, proj, vecs, qkv, dx, dres = refs[:7]
+    outs = refs[7:13]
+    sems, scratch = refs[13:16], list(refs[16:])
+    me = Where()
+    me.greet()
+    copies = Copies(*sems)
+    items = []
+
+    def take(n):
+        got = scratch[:n]
+        del scratch[:n]
+        return got
+
+    for piece in range(PIECES):
+        items.append((piece, input_grad_item(me, copies, dx, dres, piece, *take(5), outs[5])))
+    items.append((0, own_columns_item(me, copies, qkv, *take(5), outs[4])))
+    step = 0
+    for n, splits in SPLITS:
+        src = refs[n]
+        width = src.shape[4] // splits
+        for part in range(splits):
+            cols = slice(part * width, (part + 1) * width)
+            item = scatter_item(me, copies, src, cols, *take(7), outs[n].at[:, cols], step % 2 == 0)
+            items.append((step // 2, item))
+            step += 1
+    items.sort(key=lambda item: item[0])
+    run_phases(items)
+
+
+def scatter(down, up, proj, vecs, qkv, dx, dres):
+    hbm = pl.BlockSpec(memory_space=pltpu.HBM)
+    vmem = pl.BlockSpec(memory_space=pltpu.VMEM)
+    shape = jax.ShapeDtypeStruct
+    grads = (down, up, proj, vecs)
+    outs = [shape((a.shape[3] // 4, a.shape[4]), f32) for a in grads]
+    rows, cols = qkv.shape[4:]
+    outs.append(shape((4, rows // 2, cols), f32))
+    outs.append(shape(dres.shape, bf16))
+    buffers = []
+    for _ in range(PIECES):
+        tile = dres.shape[1:]
+        buffers += [
+            pltpu.VMEM((2,) + tile, bf16),
+            pltpu.VMEM((2,) + tile, bf16),
+            pltpu.VMEM(tile, bf16),
+            pltpu.VMEM(tile, f32),
+            pltpu.VMEM(tile, bf16),
+        ]
+    buffers += [
+        pltpu.VMEM((2, 2, 2, rows, cols), bf16),
+        pltpu.VMEM((2, 2, 2, rows, cols), bf16),
+        pltpu.VMEM((2, 2, rows, cols), bf16),
+        pltpu.VMEM((2, rows, cols), bf16),
+        pltpu.VMEM((2, rows, cols), f32),
+    ]
+    for n, splits in SPLITS:
+        a = grads[n]
+        for _ in range(splits):
+            buffers += scatter_buffers(a.shape[3], a.shape[4] // splits, a.dtype)
+    return pl.pallas_call(
+        scatter_kernel,
+        out_shape=tuple(outs),
+        in_specs=[hbm] * 7,
+        out_specs=(vmem,) * 5 + (hbm,),
+        scratch_shapes=[
+            pltpu.SemaphoreType.DMA((80,)),
+            pltpu.SemaphoreType.DMA((80,)),
+            pltpu.SemaphoreType.DMA((32,)),
+        ]
+        + buffers,
+        compiler_params=pltpu.CompilerParams(
+            collective_id=1, has_side_effects=True, vmem_limit_bytes=VMEM_BYTES
+        ),
+        name="scatter",
+    )(down, up, proj, vecs, qkv, dx, dres)
 
 
 def per_device(
@@ -802,28 +1025,14 @@
     thirds = g_mix[members * LANES :].reshape(members, HEAD_DIM, width)
     g_out = jnp.concatenate([pairs, thirds], axis=1).reshape(width, width)
 
-    def scatter(a):
-        return lax.psum_scatter(a, ALL, scatter_dimension=0, tiled=True).astype(f32)
-
-    g_down, g_up, g_out = scatter(g_down), scatter(g_up), scatter(g_out)
-
     draw, sums = attend_back(rand_flat, qkv, res, dctx, heads)
     dx = dot_nt(draw, w_own).astype(bf16)
-    dx = lax.psum_scatter(dx, GROUP, scatter_dimension=0, tiled=True)
-    input_grad = move((dres1 + dx.astype(f32)).astype(bf16)).astype(f32)
+    g_qkv = dot_tn(x, draw)
 
     def strip(a):
         a = a.reshape(a.shape[:-1] + (heads, 4, HEAD_DIM))
         q, k, v = a[..., 0, :] * (HEAD_DIM**-0.5), a[..., 2, :], a[..., 3, :]
         return jnp.stack([q, k, v], axis=-3).reshape(a.shape[:-3] + (3, cols))
-
-    g_qkv = strip(dot_tn(x, draw)).reshape(-1, 2, 2, members // 2, own, 3 * cols)
-    g_qkv = jnp.transpose(g_qkv, (0, 2, 1, 3, 4, 5)).reshape(-1, members, own, 3 * cols)
-    g_qkv = g_qkv.reshape(-1, 3 * cols).astype(bf16)
-    g_qkv = lax.psum_scatter(g_qkv, REST, scatter_dimension=0, tiled=True)
-    g_qkv = g_qkv.reshape(members, own, 3 * cols)
-    g_qkv = lax.all_to_all(g_qkv, GROUP, split_axis=0, concat_axis=0, tiled=True).astype(f32)
-    g_qkv = jnp.transpose(g_qkv.reshape(members, own, 3, cols), (1, 2, 0, 3)).reshape(own, -1)
 
     col_sums = strip(sums[0:1])[0]
     pair = jnp.stack([col_sums[0], col_sums[2]]).reshape(2, 1, cols)
@@ -832,7 +1041,38 @@
     vec_grads = jnp.concatenate([pair, gvec[0:6]], axis=0).reshape(8, devices, own)
     vec_grads = jnp.transpose(vec_grads, (1, 0, 2)).reshape(devices, 8 * own)
     vec_grads = jnp.concatenate([vec_grads, gbu[0].reshape(devices, -1)], axis=1)
-    vec_grads = lax.psum_scatter(vec_grads, ALL, scatter_dimension=0, tiled=True)[0]
+    count = vec_grads.shape[1]
+
+    if direct:
+        lines = 8
+        padded = jnp.pad(vec_grads, ((0, 0), (0, lines * LANES - count)))
+        g_down, g_up, g_out, vec_grads, g_qkv, input_grad = scatter(
+            g_down.reshape(2, 2, 2, -1, width),
+            g_up.reshape(2, 2, 2, -1, g_up.shape[1]),
+            g_out.reshape(2, 2, 2, -1, width),
+            padded.reshape(2, 2, 2, 4 * lines, LANES),
+            g_qkv.astype(bf16).reshape(2, 2, 2, 2, 2 * own, -1),
+            dx.reshape(2, 2, PIECES, -1, width),
+            dres1.reshape(PIECES, -1, width),
+        )
+        vec_grads = vec_grads.reshape(-1)[:count]
+        input_grad = input_grad.reshape(rows, width).astype(f32)
+        g_qkv = strip(g_qkv)
+    else:
+
+        def reduce(a):
+            return lax.psum_scatter(a, ALL, scatter_dimension=0, tiled=True).astype(f32)
+
+        g_down, g_up, g_out, vec_grads = reduce(g_down), reduce(g_up), reduce(g_out), reduce(vec_grads)[0]
+        dx = lax.psum_scatter(dx, GROUP, scatter_dimension=0, tiled=True)
+        input_grad = move((dres1 + dx.astype(f32)).astype(bf16)).astype(f32)
+        g_qkv = strip(g_qkv).reshape(-1, 2, 2, members // 2, own, 3 * cols)
+        g_qkv = jnp.transpose(g_qkv, (0, 2, 1, 3, 4, 5)).reshape(-1, members, own, 3 * cols)
+        g_qkv = g_qkv.reshape(-1, 3 * cols).astype(bf16)
+        g_qkv = lax.psum_scatter(g_qkv, REST, scatter_dimension=0, tiled=True)
+        g_qkv = g_qkv.reshape(members, own, 3 * cols)
+        g_qkv = lax.all_to_all(g_qkv, GROUP, split_axis=0, concat_axis=0, tiled=True).astype(f32)
+    g_qkv = jnp.transpose(g_qkv.reshape(members, own, 3, cols), (1, 2, 0, 3)).reshape(own, -1)
     v8 = vec_grads[: 8 * own].reshape(8, own)
     return (
         out[None],

time: 998 us -> 643 us (0.64)
  waiting for transfers between devices: 396 us -> 15 us
  Pallas kernels: 388 us -> 507 us
  blocking collectives: 64.9 us -> 0 us
  between operations: 14.1 us -> 0.93 us
    reduce_scatter x5 -> x0, waiting for transfers between devices: 377 us -> none  [the longest x3 309 us: scatter(): return lax.psum_scatter(a, ALL, scatter_dimension=0, tiled=True).astype(f32)]
    pallas_call x0 -> x1, Pallas kernels: none -> 119 us  [scatter(): pl.pallas_call(scatter_kernel, out_shape=tuple(outs), in_specs=[hbm] * 7,...]
    unnamed x1 -> x0, blocking collectives: 40.4 us -> none
    all_to_all x1 -> x0, blocking collectives: 24.5 us -> none  [per_device(): lax.all_to_all(dctx_send, GROUP, split_axis=0, concat_axis=0, tiled=True)]
  transfers between devices with their start and end apart: 10 -> 4, of which waited for: 7 -> 1; matrix products, arithmetic and copies ran while one was open for 9% -> 9% of each run, Pallas kernels for 16% -> 24%
where the time goes in v3:
time: 643 us; the launch traced here: 641 us
  Pallas kernels  507 us (79%)
  local copies, waits for them, and re-layouts  52.8 us (8%)
  matrix products  38.2 us (6%)
  starting transfers between devices  21.2 us (3%)
  waiting for transfers between devices  15 us (2%)
    pallas_call x1, Pallas kernels, gather(): pl.pallas_call(gather_kernel, out_shape=tuple(outs), in_specs=[hbm] * 7,...  155 us
    pallas_call x1, Pallas kernels, scatter(): pl.pallas_call(scatter_kernel, out_shape=tuple(outs), in_specs=[hbm] * 7,...  119 us
    pallas_call x1, Pallas kernels, attend_back(): pl.pallas_call(partial(attend_back_kernel, heads, randoms), out_shape=(ja...  95.6 us
    pallas_call x1, Pallas kernels, attend(): pl.pallas_call(partial(attend_kernel, heads, randoms), out_shape=(jax.Sha...  82.1 us
    pallas_call x1, Pallas kernels, chain(): pl.pallas_call(partial(chain_kernel, groups), grid=(rows // ROWS,), out_s...  55.4 us
    dot_general x4, matrix products, dot_tn(): return lax.dot_general(a, b, TN, preferred_element_type=f32)  30.9 us
    all_to_all x1, waiting for transfers between devices, per_device(): lax.all_to_all(ctx_send, GROUP, split_axis=0, concat_axis=0, tiled=True)  15 us
    ppermute x2, starting transfers between devices, move(): return lax.ppermute(a, ('core', 'zh'), swap)  13.9 us
  transfers between devices with their start and end apart: 4, of which 1 were waited for; matrix products, arithmetic and copies ran while one was open for 9% of the time, Pallas kernels for 24%

profile of v3, /device:TPU:0, one launch (start us, length us, event | category | flops | bytes accessed | tf_op | source)
XLA Modules:
  0.0 641.3 jit_solution(17971644558594481983)
XLA Ops:
  2.9 4.8 concatenate.20
  8.3 154.8 %gather.1 = (bf16[4,4,256,768]{3,2,1,0:T(8,128)(2,1)}, bf16[1024,768]{1,0:T(8,128)(2,1)}, bf16[2,2,2,4,24,2304]{5,4,3,2,1,0:T(8,128)(2,1)}, bf16[2,2,2,4,24,768]...) custom-call(bf16[4,256,768]{2,1,0:T(8,128)(2,1)} %bitcast.89, ...), custom_call_target="tpu_custom_call" | custom-call | tf_op jit(solution)/shard_map/gather/pallas_call | solution.py:697
  163.1 0.9 copy.55
  164.6 9.9 %reshape_reshape.12 = bf16[768,3,4,192]{3,2,1,0:T(4,128)(2,1)} reshape(bf16[2,2,2,4,24,2304]{5,4,3,2,1,0:T(8,128)(2,1)} %get-tuple-element.44) | data formatting | bytes 7077888 | tf_op jit(solution)/shard_map/reshape;reshape | solution.py:1005
  174.5 4.8 constant_dynamic-slice_fusion.1
  179.3 2.1 copy.40
  182.5 1.5 copy.45.w_ref
  184.9 82.1 %attend.1 = (bf16[4096,768]{1,0:T(8,128)(2,1)}, f32[3,4096,128]{2,1,0:T(8,128)}, bf16[4,4,384,128]{3,2,1,0:T(8,128)(2,1)}) custom-call(s32[558]{0:T(1024)} %reshape.223.rand_ref, bf16[4096,768]{1,0:T(8,128)(2,1)} %bitcast.75, bf16[768,768]{1,0:T(8,128)(2,1)} %copy.45.w_ref, f32[1,768]{1,0:T(1,128)} %reshape.229.b_ref), custom_call_target="tpu_custom_call" | custom-call | tf_op jit(solution)/shard_map/attend/pallas_call | solution.py:151
  266.9 3.7 all-to-all-start
  272.9 2.7 constant_dynamic-slice_fusion.tok_ref
  275.6 15.0 %all-to-all-done.ctx_ref = bf16[4,4,384,128]{3,2,1,0:T(8,128)(2,1)S(1)} async-done(((bf16[4,4,384,128]{3,2,1,0:T(8,128)(2,1)}), bf16[4,4,384,128]{3,2,1,0:T(8,128)(2,1)S(1)}, u32[]{:S(2)}, u32[]{:S(2)}) %all-to-all-start) | async-done | bytes 1572896 | tf_op jit(solution)/shard_map/all_to_all | solution.py:1013
  290.6 1.1 copy-done
  291.7 55.4 %chain.1 = (bf16[1024,768]{1,0:T(8,128)(2,1)}, f32[1024,768]{1,0:T(8,128)}, bf16[4,4,384,128]{3,2,1,0:T(8,128)(2,1)}, bf16[1024,768]{1,0:T(8,128)(2,1)}, bf16[10...) custom-call(bf16[4,4,384,128]{3,2,1,0:T(8,128)(2,1)} %copy-done, ...), custom_call_target="tpu_custom_call" | custom-call | tf_op jit(solution)/shard_map/chain/pallas_call | solution.py:427
  347.1 3.6 all-to-all-start.1
  351.4 13.3 %collective-permute-start.1 = (bf16[1024,768]{1,0:T(8,128)(2,1)}, bf16[1024,768]{1,0:T(8,128)(2,1)}, u32[]{:S(2)}, u32[]{:S(2)}) collective-permute-start(bf16[1024,768]{1,0:T(8,128)(2,1)} %get-tuple-element.51), channel_id=1, source_target_pairs={{0,0},{2,4},{4,2},{6,6},{1,1},{3,5},{5,3},{7,7},{8,8},{10,12},{12,... | collective-permute-start | bytes 4718600 | tf_op jit(solution)/shard_map/ppermute | solution.py:957
  364.7 9.2 %convolution_convert_fusion.2 = bf16[3072,768]{1,0:T(8,128)(2,1)} fusion(bf16[1024,3072]{1,0:T(8,128)(2,1)} %get-tuple-element.52, bf16[1024,768]{1,0:T(8,128)(2,1)} %get-tuple-element.53), kind=kOutput, calls=%fused_computation.2 | convolution fusion | flops 4834197504 | bytes 12582912 | tf_op jit(solution)/shard_map/dot_general | solution.py:40
  374.0 1.4 convolution_convert_fusion.4
  376.2 1.5 slice_reduce_fusion.4
  378.5 2.2 pad_maximum_fusion.1
  380.8 9.6 %convolution_convert_fusion.1 = bf16[768,3072]{1,0:T(8,128)(2,1)} fusion(bf16[1024,768]{1,0:T(8,128)(2,1)S(1)} %copy-done.10, bf16[1024,3072]{1,0:T(8,128)(2,1)} %get-tuple-element.55), kind=kOutput, calls=%fused_computation.1 | convolution fusion | flops 4834197504 | bytes 12582912 | tf_op jit(solution)/shard_map/dot_general | solution.py:40
  390.3 1.1 copy-done.1
  391.5 95.6 %attend_back.1 = (bf16[4096,768]{1,0:T(8,128)(2,1)}, f32[8,768]{1,0:T(8,128)}) custom-call(s32[558]{0:T(1024)} %reshape.223.rand_ref, bf16[4096,768]{1,0:T(8,128)(2,1)} %get-tuple-element.58.qkv_ref, f32[3,4096,128]{2,1,0:T(8,128)} %get-tuple-element.59.res_ref, bf16[4,4,384,128]{3,2,1,0:T(8,128)(2,1)} %copy-done.1), custom_call_target="tpu_custom_call" | custom-call | tf_op jit(solution)/shard_map/attend_back/pallas_call | solution.py:264
  487.1 10.6 %convolution_convert_fusion.3 = bf16[768,768]{1,0:T(8,128)(2,1)} fusion(bf16[4096,768]{1,0:T(8,128)(2,1)} %bitcast.77, bf16[4096,768]{1,0:T(8,128)(2,1)} %get-tuple-element.64), kind=kOutput, calls=%fused_computation.4 | convolution fusion | flops 4832428032 | bytes 13762560 | tf_op jit(solution)/shard_map/dot_general | solution.py:40
  497.7 7.3 %convolution_convert_fusion = bf16[4096,768]{1,0:T(8,128)(2,1)} fusion(bf16[4096,768]{1,0:T(8,128)(2,1)S(1)} %copy-done.9, bf16[768,768]{0,1:T(8,128)(2,1)S(1)} %bitcast.80), kind=kOutput, calls=%fused_computation | convolution fusion | flops 4834983936 | bytes 13762560 | tf_op jit(solution)/shard_map/dot_general | solution.py:36
  507.2 119.1 %scatter.1 = (f32[96,768]{1,0:T(8,128)}, f32[24,3072]{1,0:T(8,128)}, f32[24,768]{1,0:T(8,128)}, f32[8,128]{1,0:T(8,128)}, f32[4,24,768]{2,1,0:T(8,128)}, /*index=5*/bf16[4,256,768]{2,1,0:T(8,128)(2,1)}) custom-call(bf16[2,2,2,384,768]{4,3,2,1,0:T(8,128)(2,1)} %bitcast.83, bf16[2,2,2,96,3072]{4,3,2,1,0:T(8,128)(2,1)} %bitcast.84, ...), custom_call_target="tpu_custom_call" | custom-call | tf_op jit(solution)/shard_map/scatter/pallas_call | solution.py:917
  626.3 1.3 slice.161
  628.2 1.5 fusion.7
  630.3 1.2 reshape.244
  631.6 1.4 fusion.1
  633.7 0.9 reshape.245
  634.6 1.9 bitcast_convert_fusion
  636.5 2.7 copy.61
  (89 shorter events, 16.2 us)
Async XLA Ops:
  1.3 182.6 %collective-permute-start = (s32[3,62,3]{1,2,0:T(4,128)S(1)}, s32[3,62,3]{1,2,0:T(4,128)S(1)}, u32[]{:S(2)}, u32[]{:S(2)}) collective-permute-start(s32[3,62,3]{1,2,0:T(4,128)S(1)} %bitcast.100), channel_id=1, source_target_pairs={{0,0},{2,4},{4,2},{6,6},{1,1},{3,5},{5,3},{7,7},{8,8},{10,12},{12,... | collective-permute-start | bytes 6704 | tf_op jit(solution)/shard_map/ppermute | solution.py:957
  266.9 23.6 %all-to-all-start = ((bf16[4,4,384,128]{3,2,1,0:T(8,128)(2,1)}), bf16[4,4,384,128]{3,2,1,0:T(8,128)(2,1)S(1)}, u32[]{:S(2)}, u32[]{:S(2)}) async-start(bf16[4,4,384,128]{3,2,1,0:T(8,128)(2,1)} %get-tuple-element.46), calls=%async_computation | async-start | bytes 3145728 | tf_op jit(solution)/shard_map/all_to_all | solution.py:1013
  290.6 1.1 copy-start
  347.1 3.6 copy-start.7
  347.1 43.2 %all-to-all-start.1 = ((bf16[4,4,384,128]{3,2,1,0:T(8,128)(2,1)}), bf16[4,4,384,128]{3,2,1,0:T(8,128)(2,1)S(1)}, u32[]{:S(2)}, u32[]{:S(2)}) async-start(bf16[4,4,384,128]{3,2,1,0:T(8,128)(2,1)} %get-tuple-element.60), calls=%async_computation.1 | async-start | bytes 3145728 | tf_op jit(solution)/shard_map/all_to_all | solution.py:1018
  351.4 38.9 %collective-permute-start.1 = (bf16[1024,768]{1,0:T(8,128)(2,1)}, bf16[1024,768]{1,0:T(8,128)(2,1)}, u32[]{:S(2)}, u32[]{:S(2)}) collective-permute-start(bf16[1024,768]{1,0:T(8,128)(2,1)} %get-tuple-element.51), channel_id=1, source_target_pairs={{0,0},{2,4},{4,2},{6,6},{1,1},{3,5},{5,3},{7,7},{8,8},{10,12},{12,... | collective-permute-start | bytes 4718600 | tf_op jit(solution)/shard_map/ppermute | solution.py:957
  364.7 9.3 %copy-start.11 = (bf16[1024,768]{1,0:T(8,128)(2,1)S(1)}, bf16[1024,768]{1,0:T(8,128)(2,1)}, u32[]{:S(2)}) copy-start(bf16[1024,768]{1,0:T(8,128)(2,1)} %get-tuple-element.56) | copy-start | bytes 4718596
  364.7 9.3 %copy-start.12 = (bf16[1024,768]{1,0:T(8,128)(2,1)S(1)}, bf16[1024,768]{1,0:T(8,128)(2,1)}, u32[]{:S(2)}) copy-start(bf16[1024,768]{1,0:T(8,128)(2,1)} %get-tuple-element.57) | copy-start | bytes 4718596
  378.5 2.2 copy-start.10
  390.3 1.1 copy-start.1
  487.1 10.6 %copy-start.9 = (bf16[4096,768]{1,0:T(8,128)(2,1)S(1)}, bf16[4096,768]{1,0:T(8,128)(2,1)}, u32[]{:S(2)}) copy-start(bf16[4096,768]{1,0:T(8,128)(2,1)} %get-tuple-element.64) | copy-start | bytes 18874372
  497.7 8.4 %copy-start.8 = (pred[32]{0:T(512)(128)(4,1)S(1)}, pred[32]{0:T(512)(128)(4,1)}, u32[]{:S(2)}) copy-start(pred[32]{0:T(512)(128)(4,1)} %broadcast_in_dim.34) | copy-start | bytes 100
  497.7 8.5 %copy-start.3 = (f32[6,32,24]{2,1,0:T(8,128)S(1)}, f32[6,32,24]{2,1,0:T(8,128)}, u32[]{:S(2)}) copy-start(f32[6,32,24]{2,1,0:T(8,128)} %concatenate.23) | copy-start | bytes 55300
  631.6 3.0 copy-start.2
  636.5 2.7 copy-start.6
  636.5 3.4 copy-start.5
  636.5 4.1 copy-start.4

commit v4 on v3

--- a/solution.py
+++ b/solution.py
@@ -20,6 +20,8 @@
 REST = ("c", "zh")
 CHUNK = 512
 ROWS = 256
+PAIR = 2
+PAIR_BACK = 2
 VMEM_BYTES = 60 * 1024 * 1024
 
 f32 = jnp.float32
@@ -44,16 +46,19 @@
     return pl.ds(pl.multiple_of(start, size), size)
 
 
-def listed(ref, rand_ref, head, i, blocks, randoms, cols):
-    parts = [
-        ref[0:BLOCK, cols],
-        ref[(blocks - 1) * BLOCK : blocks * BLOCK, cols],
-        ref[pl.ds(pl.multiple_of((i - 1) * BLOCK, BLOCK), 3 * BLOCK), cols],
-    ]
-    base = (head * (blocks - 2) + i - 1) * randoms
-    for r in range(randoms):
-        parts.append(ref[rows_at(rand_ref[base + r] * BLOCK, BLOCK), cols])
+def listed(ref, rand_ref, head, i, blocks, randoms):
+    cols = slice(head * SLOT + LANES, head * SLOT + SLOT)
+    near = jnp.clip(i - 1, 0, blocks - 3)
+    parts = [ref[0, :, cols], ref[blocks - 1, :, cols]]
+    parts += [ref[near + n, :, cols] for n in range(3)]
+    base = (head * (blocks - 2) + near) * randoms
+    parts += [ref[rand_ref[base + r], :, cols] for r in range(randoms)]
     return jnp.concatenate(parts, axis=0)
+
+
+def keys_values(ref, head, t, size):
+    cols = slice(head * SLOT + LANES, head * SLOT + SLOT)
+    return ref[pl.ds(t * (size // BLOCK), size // BLOCK), :, cols].reshape(size, LANES)
 
 
 def mask_globals(s, i, blocks):
@@ -63,82 +68,92 @@
     return jnp.concatenate([jnp.where(dead, MASKED, s[:, :LANES]), s[:, LANES:]], axis=1)
 
 
+def middle_blocks(qkv_ref, rand_ref, res_ref, first, heads, randoms, blocks):
+    lane = lax.broadcasted_iota(jnp.int32, (BLOCK, LANES), 1)
+    work = [(first + n, h) for n in range(PAIR) for h in range(heads)]
+    kvs = [listed(qkv_ref, rand_ref, h, i, blocks, randoms) for i, h in work]
+    qs = [qkv_ref[i, :, h * SLOT : h * SLOT + LANES] for i, h in work]
+    ss = [mask_globals(dot_nt(q, kv), i, blocks) for q, kv, (i, h) in zip(qs, kvs, work)]
+    tops = [jnp.max(s, axis=1, keepdims=True) for s in ss]
+    es = [jnp.exp(s - top) for s, top in zip(ss, tops)]
+    totals = [jnp.sum(e, axis=1, keepdims=True) for e in es]
+    os = [dot(e.astype(bf16), kv) for e, kv in zip(es, kvs)]
+    for o, top, total, (i, h) in zip(os, tops, totals, work):
+        both = jnp.where(lane < HEAD_DIM, top + jnp.log(total), o / total)
+        res_ref[h, rows_at(i * BLOCK, BLOCK), :] = both
+
+
+def global_blocks(qkv_ref, heads, length):
+    last = length // BLOCK - 1
+
+    def ends(h):
+        cols = slice(h * SLOT, h * SLOT + LANES)
+        return jnp.concatenate([qkv_ref[0, :, cols], qkv_ref[last, :, cols]], axis=0)
+
+    qs = [ends(h) for h in range(heads)]
+
+    def whole(t, carry):
+        kvs = [keys_values(qkv_ref, h, t, CHUNK) for h in range(heads)]
+        ss = [dot_nt(q, kv) for q, kv in zip(qs, kvs)]
+        news = [jnp.maximum(c[0], jnp.max(s, axis=1, keepdims=True)) for c, s in zip(carry, ss)]
+        fades = [jnp.exp(c[0] - new) for c, new in zip(carry, news)]
+        es = [jnp.exp(s - new) for s, new in zip(ss, news)]
+        sums = [jnp.sum(e, axis=1, keepdims=True) for e in es]
+        os = [dot(e.astype(bf16), kv) for e, kv in zip(es, kvs)]
+        return tuple(
+            (new, c[1] * fade + total, c[2] * fade + o)
+            for c, new, fade, total, o in zip(carry, news, fades, sums, os)
+        )
+
+    start = (
+        jnp.full((2 * BLOCK, 1), MASKED, f32),
+        jnp.zeros((2 * BLOCK, 1), f32),
+        jnp.zeros((2 * BLOCK, LANES), f32),
+    )
+    done = lax.fori_loop(0, length // CHUNK, whole, (start,) * heads)
+    lane = lax.broadcasted_iota(jnp.int32, (2 * BLOCK, LANES), 1)
+    return [jnp.where(lane < HEAD_DIM, top + jnp.log(total), acc / total) for top, total, acc in done]
+
+
+def pack_rows(res_ref, ctx_ref, start, part, piece):
+    low = lax.broadcasted_iota(jnp.int32, (BLOCK, LANES), 1) < HEAD_DIM
+    for n in range(ROWS // BLOCK):
+        rows = rows_at(start + n * BLOCK, BLOCK)
+        first = pltpu.roll(res_ref[0, rows, :], HEAD_DIM, 1)
+        pair = jnp.where(low, first, res_ref[1, rows, :])
+        ctx_ref[part, piece, n * BLOCK : (n + 1) * BLOCK, :] = pair.astype(bf16)
+    for n in range(ROWS // (2 * BLOCK)):
+        rows = rows_at(start + 2 * n * BLOCK, BLOCK)
+        odd = rows_at(start + (2 * n + 1) * BLOCK, BLOCK)
+        first = pltpu.roll(res_ref[2, rows, :], HEAD_DIM, 1)
+        both = jnp.where(low, first, res_ref[2, odd, :])
+        ctx_ref[part, piece, ROWS + n * BLOCK : ROWS + (n + 1) * BLOCK, :] = both.astype(bf16)
+
+
 def attend_kernel(heads, randoms, rand_ref, x_ref, w_ref, b_ref, qkv_ref, res_ref, ctx_ref):
     length = x_ref.shape[0]
     blocks = length // BLOCK
-    last = (blocks - 1) * BLOCK
 
     def project(t, carry):
-        rows = rows_at(t * CHUNK, CHUNK)
-        qkv_ref[rows, :] = (dot(x_ref[rows, :], w_ref[...]) + b_ref[...]).astype(bf16)
+        raw = dot(x_ref[rows_at(t * CHUNK, CHUNK), :], w_ref[...]) + b_ref[...]
+        step = CHUNK // BLOCK
+        qkv_ref[pl.ds(t * step, step)] = raw.astype(bf16).reshape(step, BLOCK, raw.shape[1])
         return carry
 
     lax.fori_loop(0, length // CHUNK, project, 0)
 
-    def middle(i, carry):
-        rows = rows_at(i * BLOCK, BLOCK)
-        lane = lax.broadcasted_iota(jnp.int32, (BLOCK, LANES), 1)
-        for h in range(heads):
-            at = h * SLOT
-            kv = listed(qkv_ref, rand_ref, h, i, blocks, randoms, slice(at + LANES, at + SLOT))
-            s = mask_globals(dot_nt(qkv_ref[rows, at : at + LANES], kv), i, blocks)
-            top = jnp.max(s, axis=1, keepdims=True)
-            e = jnp.exp(s - top)
-            total = jnp.sum(e, axis=1, keepdims=True)
-            o = dot(e.astype(bf16), kv) / total
-            res_ref[h, rows, :] = jnp.where(lane < HEAD_DIM, top + jnp.log(total), o)
+    def middle(t, carry):
+        middle_blocks(qkv_ref, rand_ref, res_ref, t * PAIR, heads, randoms, blocks)
         return carry
 
-    lax.fori_loop(1, blocks - 1, middle, 0)
-
-    for h in range(heads):
-        at = h * SLOT
-        q = jnp.concatenate(
-            [qkv_ref[0:BLOCK, at : at + LANES], qkv_ref[last : last + BLOCK, at : at + LANES]], axis=0
-        )
-
-        def whole(t, carry, at=at, q=q):
-            top, total, acc = carry
-            kv = qkv_ref[rows_at(t * CHUNK, CHUNK), at + LANES : at + SLOT]
-            s = dot_nt(q, kv)
-            new = jnp.maximum(top, jnp.max(s, axis=1, keepdims=True))
-            fade = jnp.exp(top - new)
-            e = jnp.exp(s - new)
-            total = total * fade + jnp.sum(e, axis=1, keepdims=True)
-            return new, total, acc * fade + dot(e.astype(bf16), kv)
-
-        top, total, acc = lax.fori_loop(
-            0,
-            length // CHUNK,
-            whole,
-            (
-                jnp.full((2 * BLOCK, 1), MASKED, f32),
-                jnp.zeros((2 * BLOCK, 1), f32),
-                jnp.zeros((2 * BLOCK, LANES), f32),
-            ),
-        )
-        lane = lax.broadcasted_iota(jnp.int32, (2 * BLOCK, LANES), 1)
-        both = jnp.where(lane < HEAD_DIM, top + jnp.log(total), acc / total)
+    lax.fori_loop(0, blocks // PAIR, middle, 0)
+    for h, both in enumerate(global_blocks(qkv_ref, heads, length)):
         res_ref[h, 0:BLOCK, :] = both[:BLOCK]
-        res_ref[h, last : last + BLOCK, :] = both[BLOCK:]
-
+        res_ref[h, length - BLOCK : length, :] = both[BLOCK:]
     per_quarter = ctx_ref.shape[1]
 
     def pack(t, carry):
-        part, piece = t // per_quarter, t % per_quarter
-        lane = lax.broadcasted_iota(jnp.int32, (BLOCK, LANES), 1)
-        low = lane < HEAD_DIM
-        for n in range(ROWS // BLOCK):
-            rows = rows_at(t * ROWS + n * BLOCK, BLOCK)
-            first = pltpu.roll(res_ref[0, rows, :], HEAD_DIM, 1)
-            pair = jnp.where(low, first, res_ref[1, rows, :])
-            ctx_ref[part, piece, n * BLOCK : (n + 1) * BLOCK, :] = pair.astype(bf16)
-        for n in range(ROWS // (2 * BLOCK)):
-            rows = rows_at(t * ROWS + 2 * n * BLOCK, BLOCK)
-            odd = rows_at(t * ROWS + (2 * n + 1) * BLOCK, BLOCK)
-            first = pltpu.roll(res_ref[2, rows, :], HEAD_DIM, 1)
-            both = jnp.where(low, first, res_ref[2, odd, :])
-            ctx_ref[part, piece, ROWS + n * BLOCK : ROWS + (n + 1) * BLOCK, :] = both.astype(bf16)
+        pack_rows(res_ref, ctx_ref, t * ROWS, t // per_quarter, t % per_quarter)
         return carry
 
     lax.fori_loop(0, length // ROWS, pack, 0)
@@ -151,7 +166,7 @@
     return pl.pallas_call(
         partial(attend_kernel, heads, randoms),
         out_shape=(
-            jax.ShapeDtypeStruct((length, heads * SLOT), bf16),
+            jax.ShapeDtypeStruct((length // BLOCK, BLOCK, heads * SLOT), bf16),
             jax.ShapeDtypeStruct((heads, length, LANES), f32),
             jax.ShapeDtypeStruct((parts, length // parts // ROWS, ROWS * 3 // 2, LANES), bf16),
         ),
@@ -166,8 +181,8 @@
     heads, randoms, rand_ref, qkv_ref, res_ref, dctx_ref, draw_ref, sums_ref, *scratch
 ):
     dout, acc = scratch[:heads], scratch[heads:]
-    length = qkv_ref.shape[0]
-    blocks = length // BLOCK
+    blocks = qkv_ref.shape[0]
+    length = blocks * BLOCK
     last = (blocks - 1) * BLOCK
     per_quarter = dctx_ref.shape[1]
 
@@ -191,48 +206,73 @@
     lax.fori_loop(0, length // ROWS, unpack, 0)
 
     step = 256
+
+    def ends(ref, cols):
+        return jnp.concatenate([ref[0:BLOCK, cols], ref[last : last + BLOCK, cols]], axis=0)
+
+    every = slice(0, LANES)
+    gs = [ends(dout[h], every) for h in range(heads)]
+    reses = [ends(res_ref.at[h], every) for h in range(heads)]
+    alls = [
+        jnp.concatenate(
+            [qkv_ref[n, :, h * SLOT : h * SLOT + LANES] for n in (0, blocks - 1)] + [gs[h]], axis=0
+        )
+        for h in range(heads)
+    ]
+    logs = [res[:, 0:1] for res in reses]
+    deltas = [jnp.sum(g.astype(f32) * res, axis=1, keepdims=True) for g, res in zip(gs, reses)]
+
+    def whole(t, dqs):
+        rows = rows_at(t * step, step)
+        kvs = [keys_values(qkv_ref, h, t, step) for h in range(heads)]
+        sds = [dot_nt(both, kv) for both, kv in zip(alls, kvs)]
+        ps = [jnp.exp(sd[: 2 * BLOCK] - log) for sd, log in zip(sds, logs)]
+        dss = [(p * (sd[2 * BLOCK :] - d)).astype(bf16) for p, sd, d in zip(ps, sds, deltas)]
+        dkvs = [
+            dot_tn(jnp.concatenate([ds, p.astype(bf16)], axis=0), both)
+            for ds, p, both in zip(dss, ps, alls)
+        ]
+        news = tuple(dq + dot(ds, kv) for dq, ds, kv in zip(dqs, dss, kvs))
+        for h in range(heads):
+            acc[h][rows, :] = dkvs[h]
+        return news
+
+    dqs = lax.fori_loop(
+        0, length // step, whole, (jnp.zeros((2 * BLOCK, LANES), f32),) * heads
+    )
     for h in range(heads):
-        at = h * SLOT
-        q = jnp.concatenate(
-            [qkv_ref[0:BLOCK, at : at + LANES], qkv_ref[last : last + BLOCK, at : at + LANES]], axis=0
-        )
-        g = jnp.concatenate([dout[h][0:BLOCK, :], dout[h][last : last + BLOCK, :]], axis=0)
-        res = jnp.concatenate([res_ref[h, 0:BLOCK, :], res_ref[h, last : last + BLOCK, :]], axis=0)
-        log_total = res[:, 0:1]
-        delta = jnp.sum(g.astype(f32) * res, axis=1, keepdims=True)
-        both = jnp.concatenate([q, g], axis=0)
-
-        def whole(t, dq, at=at, h=h, both=both, log_total=log_total, delta=delta):
-            rows = rows_at(t * step, step)
-            kv = qkv_ref[rows, at + LANES : at + SLOT]
-            sd = dot_nt(both, kv)
-            p = jnp.exp(sd[: 2 * BLOCK] - log_total)
-            ds = (p * (sd[2 * BLOCK :] - delta)).astype(bf16)
-            acc[h][rows, :] = dot_tn(jnp.concatenate([ds, p.astype(bf16)], axis=0), both)
-            return dq + dot(ds, kv)
-
-        dq = lax.fori_loop(0, length // step, whole, jnp.zeros((2 * BLOCK, LANES), f32))
+        cols = slice(h * SLOT, h * SLOT + LANES)
         lane = lax.broadcasted_iota(jnp.int32, (2 * BLOCK, LANES), 1)
-        dq = jnp.where(lane < HEAD_DIM, dq, 0.0).astype(bf16)
-        draw_ref[0:BLOCK, at : at + LANES] = dq[:BLOCK]
-        draw_ref[last : last + BLOCK, at : at + LANES] = dq[BLOCK:]
-
-    def middle(i, carry):
-        rows = rows_at(i * BLOCK, BLOCK)
+        dq = jnp.where(lane < HEAD_DIM, dqs[h], 0.0).astype(bf16)
+        draw_ref[0:BLOCK, cols] = dq[:BLOCK]
+        draw_ref[last : last + BLOCK, cols] = dq[BLOCK:]
+
+    def middle(t, carry):
         lane = lax.broadcasted_iota(jnp.int32, (BLOCK, LANES), 1)
-        for h in range(heads):
-            at = h * SLOT
-            kv = listed(qkv_ref, rand_ref, h, i, blocks, randoms, slice(at + LANES, at + SLOT))
-            g = dout[h][rows, :]
-            res = res_ref[h, rows, :]
-            both = jnp.concatenate([qkv_ref[rows, at : at + LANES], g], axis=0)
-            delta = jnp.sum(g.astype(f32) * res, axis=1, keepdims=True)
-            sd = dot_nt(both, kv)
-            p = jnp.exp(mask_globals(sd[:BLOCK], i, blocks) - res[:, 0:1])
-            ds = (p * (sd[BLOCK:] - delta)).astype(bf16)
-            dkv = dot_tn(jnp.concatenate([ds, p.astype(bf16)], axis=0), both)
-            dq = dot(ds, kv)
-            draw_ref[rows, at : at + LANES] = jnp.where(lane < HEAD_DIM, dq, 0.0).astype(bf16)
+        work = [(1 + t * PAIR_BACK + n, h) for n in range(PAIR_BACK) for h in range(heads)]
+        kvs = [listed(qkv_ref, rand_ref, h, i, blocks, randoms) for i, h in work]
+        places = [(rows_at(i * BLOCK, BLOCK), slice(h * SLOT, h * SLOT + LANES)) for i, h in work]
+        gs = [dout[h][rows, :] for (rows, _), (_, h) in zip(places, work)]
+        reses = [res_ref[h, rows, :] for (rows, _), (_, h) in zip(places, work)]
+        alls = [
+            jnp.concatenate([qkv_ref[i, :, cols], g], axis=0)
+            for (_, cols), (i, _), g in zip(places, work, gs)
+        ]
+        sds = [dot_nt(both, kv) for both, kv in zip(alls, kvs)]
+        deltas = [jnp.sum(g.astype(f32) * res, axis=1, keepdims=True) for g, res in zip(gs, reses)]
+        ps = [
+            jnp.exp(mask_globals(sd[:BLOCK], i, blocks) - res[:, 0:1])
+            for sd, res, (i, h) in zip(sds, reses, work)
+        ]
+        dss = [(p * (sd[BLOCK:] - d)).astype(bf16) for p, sd, d in zip(ps, sds, deltas)]
+        dkvs = [
+            dot_tn(jnp.concatenate([ds, p.astype(bf16)], axis=0), both)
+            for ds, p, both in zip(dss, ps, alls)
+        ]
+        dqs = [dot(ds, kv) for ds, kv in zip(dss, kvs)]
+        for dq, (rows, cols) in zip(dqs, places):
+            draw_ref[rows, cols] = jnp.where(lane < HEAD_DIM, dq, 0.0).astype(bf16)
+        for dkv, (i, h) in zip(dkvs, work):
             acc[h][0:BLOCK, :] += dkv[0:BLOCK]
             acc[h][last : last + BLOCK, :] += dkv[BLOCK : 2 * BLOCK]
             near = pl.ds(pl.multiple_of((i - 1) * BLOCK, BLOCK), 3 * BLOCK)
@@ -243,7 +283,7 @@
                 acc[h][far, :] += dkv[(5 + r) * BLOCK : (6 + r) * BLOCK]
         return carry
 
-    lax.fori_loop(1, blocks - 1, middle, 0)
+    lax.fori_loop(0, (blocks - 2) // PAIR_BACK, middle, 0)
     sums_ref[...] = jnp.zeros_like(sums_ref)
 
     def finish(t, carry):
@@ -258,7 +298,7 @@
 
 
 def attend_back(rand, qkv, res, dctx, heads):
-    length = qkv.shape[0]
+    length = qkv.shape[0] * BLOCK
     randoms = rand.size // (heads * (length // BLOCK - 2))
     vmem = pl.BlockSpec(memory_space=pltpu.VMEM)
     return pl.pallas_call(
@@ -661,54 +701,211 @@
 PIECES = 4
 
 
-def gather_kernel(
-    tok, og, qkv, w_out, up, down, small, x_all, og_all, qkv_all, out_all, up_all, down_all, small_all, *sems
-):
+def weight_item(me, copies, src, parts, whole, bias):
+    y, x, core, zh, zl = me.y, me.x, me.core, me.zh, me.zl
+    place = core * 2 + zl
+    keep = copies.local(src.at[place], parts.at[place])
+    moves = [
+        copies.remote(src.at[core * 2 + 1 - zl], parts.at[place], me.by_zl),
+        copies.remote(src.at[(1 - core) * 2 + zl], parts.at[place], me.by_core),
+        copies.remote(src.at[(1 - core) * 2 + 1 - zl], parts.at[place], me.by_both),
+    ]
+    keep.start()
+    for move in moves:
+        move.start()
+    yield 1
+    keep.wait()
+    for move in moves:
+        move.wait()
+    own = whole.shape[4] // 2
+    for b in range(2):
+        both = jnp.concatenate([parts[2 * b, :own, :], parts[2 * b + 1, :own, :]], axis=0)
+        whole[y, x, b, zh] = both.astype(bf16)
+    tail = pl.ds(own, 8)
+    bias[y, x, zh] = parts[0, tail, :] + parts[1, tail, :] + parts[2, tail, :] + parts[3, tail, :]
+    for spot, bias_spot, other in (
+        (whole.at[y, x, :, zh], bias.at[y, x, zh], me.by_zh),
+        (whole.at[y, x], bias.at[y, x], me.by_x),
+        (whole.at[y], bias.at[y], me.by_y),
+    ):
+        moves = [copies.remote(spot, spot, other), copies.remote(bias_spot, bias_spot, other)]
+        for move in moves:
+            move.start()
+        yield 1
+        for move in moves:
+            move.wait()
+
+
+def finish(*generators):
+    for phases in generators:
+        for _ in phases:
+            pass
+
+
+def front_kernel(heads, randoms, *refs):
+    rand_ref, tok, og, wq, w_out, up, down, small = refs[:8]
+    x_hbm, tok_own, og_own, w_own, qkv_hbm, res_hbm, ctx_all, out_all, up_all, down_all, small_all = refs[8:19]
+    x_all, parts, whole, bias, qkv_ref, res_ref, ends_ref, ctx_ref = refs[19:27]
     me = Where()
     me.greet()
-    copies = Copies(*sems)
-    items = []
-
-    def halves(first, shard, full):
-        half = shard.shape[1] // 2
-        for n in range(2):
-            items.append((first, gather_item(me, copies, shard, full, slice(n * half, (n + 1) * half), n == 0)))
-
-    items.append((0, gather_item(me, copies, small, small_all, slice(0, LANES), True)))
-    for piece in range(PIECES):
-        items.append((piece, tokens_item(me, copies, tok, x_all, piece)))
-        if piece == 0:
-            halves(0, qkv, qkv_all)
-    halves(1, w_out, out_all)
-    halves(2, up, up_all)
-    halves(3, down, down_all)
-    items.append((4, exchange_item(me, copies, og, og_all)))
-    items.sort(key=lambda item: item[0])
-    run_phases(items)
-
-
-def gather(tok, og, mats, small, members):
+    copies = Copies(*refs[27:])
+    blocks = qkv_ref.shape[0]
+    length = blocks * BLOCK
+    quarter = length // 4
+    core, zl = me.core, me.zl
+    place = core * 2 + zl
+    near = core * 2 + 1 - zl
+    beside = (1 - core) * 2 + zl
+    across = (1 - core) * 2 + 1 - zl
+
+    weights = weight_item(me, copies, wq, parts, whole, bias)
+    tokens = [tokens_item(me, copies, tok, x_all, piece) for piece in range(PIECES)]
+    smalls = gather_item(me, copies, small, small_all, slice(0, LANES), True)
+    later = []
+    turn = 0
+    for shard, full, splits, first in ((w_out, out_all, 1, 0), (up, up_all, 4, 0), (down, down_all, 2, 1)):
+        width = shard.shape[1] // splits
+        for n in range(splits):
+            cols = slice(n * width, (n + 1) * width)
+            later.append((first + n, gather_item(me, copies, shard, full, cols, turn % 2 == 0)))
+            turn += 1
+    later.append((4, exchange_item(me, copies, og, og_own)))
+    later.append((1, smalls))
+    state = {"step": 0, "live": later}
+
+    def advance():
+        after = []
+        for first, phases in state["live"]:
+            if first > state["step"] or next(phases, None) is not None:
+                after.append((first, phases))
+        state["live"] = after
+        state["step"] += 1
+
+    outs = []
+
+    def write(src, dst):
+        copy = copies.local(src, dst)
+        copy.start()
+        outs.append(copy)
+
+    def project(where):
+        bias_row = jnp.sum(bias[...].reshape(-1, 8, bias.shape[-1]), axis=0)[0:1]
+        matrix = whole[...].reshape(-1, whole.shape[-1])
+        for piece in range(PIECES):
+            raw = dot(x_all[where, piece], matrix) + bias_row
+            step = ROWS // BLOCK
+            at = (where * PIECES + piece) * step
+            qkv_ref[pl.ds(at, step)] = raw.astype(bf16).reshape(step, BLOCK, raw.shape[1])
+
+    next(weights)
+    for item in tokens:
+        next(item)
+    next(weights)
+    for item in tokens:
+        next(item)
+    next(weights)
+    next(weights)
+    finish(weights)
+    write(whole, w_own)
+    write(x_all.at[place], tok_own)
+    project(place)
+    for item in tokens:
+        next(item)
+    advance()
+    project(near)
+    finish(*tokens)
+    project(beside)
+    advance()
+    project(across)
+    write(x_all, x_hbm)
+    write(qkv_ref, qkv_hbm)
+    for h, both in enumerate(global_blocks(qkv_ref, heads, length)):
+        ends_ref[h] = both
+    advance()
+
+    def middle(t, carry):
+        middle_blocks(qkv_ref, rand_ref, res_ref, t * PAIR, heads, randoms, blocks)
+        return carry
+
+    sends = []
+    turns = quarter // BLOCK // PAIR
+    for where, other in ((across, me.by_both), (near, me.by_zl), (beside, me.by_core), (place, None)):
+        half = turns // 2
+        lax.fori_loop(where * turns, where * turns + half, middle, 0)
+        advance()
+        lax.fori_loop(where * turns + half, (where + 1) * turns, middle, 0)
+
+        @pl.when(where == 0)
+        def _():
+            for h in range(heads):
+                res_ref[h, 0:BLOCK, :] = ends_ref[h, 0:BLOCK, :]
+
+        @pl.when(where == 3)
+        def _():
+            for h in range(heads):
+                res_ref[h, length - BLOCK : length, :] = ends_ref[h, BLOCK : 2 * BLOCK, :]
+
+        for piece in range(PIECES):
+            pack_rows(res_ref, ctx_ref, where * quarter + piece * ROWS, where, piece)
+        rows = rows_at(where * quarter, quarter)
+        write(res_ref.at[:, rows], res_hbm.at[:, rows])
+        if other is None:
+            write(ctx_ref.at[where], ctx_all.at[place])
+        else:
+            send = copies.remote(ctx_ref.at[where], ctx_all.at[place], other)
+            send.start()
+            sends.append(send)
+        advance()
+    while state["live"]:
+        advance()
+    for copy in sends + outs:
+        copy.wait()
+
+
+def front(rand, tok, og, wq, mats, small, heads):
     rows, width = tok.shape
+    members = 4
+    length = rows * members
+    randoms = rand.size // (heads * (length // BLOCK - 2))
     hbm = pl.BlockSpec(memory_space=pltpu.HBM)
     shape = jax.ShapeDtypeStruct
     tok = tok.reshape(PIECES, rows // PIECES, width)
-    outs = [shape((members,) + tok.shape, bf16), shape(og.shape, bf16)]
+    cols = heads * SLOT
+    own = mats[0].shape[0]
+    packed = (members, rows // ROWS, ROWS * 3 // 2, LANES)
+    outs = [
+        shape((members,) + tok.shape, bf16),
+        shape(tok.shape, bf16),
+        shape(og.shape, bf16),
+        shape((2, 2, 2, 2, 2 * own, cols), bf16),
+        shape((length // BLOCK, BLOCK, cols), bf16),
+        shape((heads, length, LANES), f32),
+        shape(packed, bf16),
+    ]
     outs += [shape((2, 2, 2, 4) + a.shape, bf16) for a in (*mats, small)]
     return pl.pallas_call(
-        gather_kernel,
+        partial(front_kernel, heads, randoms),
         out_shape=tuple(outs),
-        in_specs=[hbm] * 7,
-        out_specs=(hbm,) * 7,
+        in_specs=[pl.BlockSpec(memory_space=pltpu.SMEM)] + [hbm] * 7,
+        out_specs=(hbm,) * 11,
         scratch_shapes=[
+            pltpu.VMEM((members,) + tok.shape, bf16),
+            pltpu.VMEM(wq.shape, f32),
+            pltpu.VMEM((2, 2, 2, 2, 2 * own, cols), bf16),
+            pltpu.VMEM((2, 2, 2, 8, cols), f32),
+            pltpu.VMEM((length // BLOCK, BLOCK, cols), bf16),
+            pltpu.VMEM((heads, length, LANES), f32),
+            pltpu.VMEM((heads, 2 * BLOCK, LANES), f32),
+            pltpu.VMEM(packed, bf16),
             pltpu.SemaphoreType.DMA((112,)),
             pltpu.SemaphoreType.DMA((112,)),
-            pltpu.SemaphoreType.DMA((16,)),
+            pltpu.SemaphoreType.DMA((32,)),
         ],
         compiler_params=pltpu.CompilerParams(
             collective_id=0, has_side_effects=True, vmem_limit_bytes=VMEM_BYTES
         ),
-        name="gather",
-    )(tok, og, *mats, small)
+        name="front",
+    )(rand, tok, og, wq, *mats, small)
 
 
 def add_rows(dst, a, b, rows):
@@ -962,37 +1159,7 @@
     cols = heads * HEAD_DIM
     group = lax.axis_index(GROUP)
     own = width // devices
-    small = jnp.concatenate(
-        [
-            query_value_bias[0],
-            query_value_bias[1],
-            out_bias,
-            norm1_gain,
-            norm1_bias,
-            down_bias,
-            norm2_gain,
-            norm2_bias,
-            up_bias,
-        ]
-    )
-    mats = (qkv_weight, out_weight, up_weight, down_weight)
-    direct = lax.axis_size("c") == 4 and members == 4 and own % 8 == 0
-    if direct:
-        count = small.shape[0]
-        padded = jnp.pad(small, (0, 16 * LANES - count)).reshape(16, LANES)
-        x, og, *full, small = gather(tokens[0], out_grad[0], mats, padded, members)
-        x = x.reshape(members * rows, width)
-        tok = lax.dynamic_slice_in_dim(x, group * rows, rows, axis=0)
-        w_qkv, w_out, w_up, w_down = (a.reshape(-1, a.shape[-1]) for a in full)
-        small = small.reshape(devices, -1)[:, :count].astype(f32)
-    else:
-        tok = move(tokens[0])
-        og = move(out_grad[0])
-        x = lax.all_gather(tok, GROUP, axis=0, tiled=True)
-        w_qkv, w_out, w_up, w_down = (lax.all_gather(a, ALL, axis=0, tiled=True) for a in mats)
-        small = lax.all_gather(small, ALL, axis=0).astype(f32)
-    vecs = jnp.transpose(small[:, : 8 * own].reshape(devices, 8, own), (1, 0, 2)).reshape(8, width)
-    bias_up = small[:, 8 * own :].reshape(1, -1)
+    rand_flat = rand.reshape(-1)
 
     def lay_out(a):
         a = a.reshape(a.shape[:-2] + (3, heads, HEAD_DIM))
@@ -1001,17 +1168,45 @@
         laid = jnp.stack([q, jnp.zeros_like(q), k, v], axis=-2)
         return laid.reshape(laid.shape[:-3] + (heads * SLOT,))
 
-    w_own = lax.dynamic_slice_in_dim(
-        w_qkv.reshape(width, 3, members, cols), group, 1, axis=2
-    ).reshape(width, 3, cols)
-    w_own = lay_out(w_own)
-    bias3 = jnp.stack([vecs[0], jnp.zeros_like(vecs[0]), vecs[1]]).reshape(3, members, cols)
-    b_own = lay_out(lax.dynamic_slice_in_dim(bias3, group, 1, axis=1).reshape(1, 3, cols))
-    rand_flat = rand.reshape(-1)
-
-    qkv, res, ctx_send = attend(rand_flat, x, w_own, b_own, members, heads)
-    ctx = lax.all_to_all(ctx_send, GROUP, split_axis=0, concat_axis=0, tiled=True)
-    chain_vecs = jnp.concatenate([vecs[2:8], jnp.zeros((2, width), f32)], axis=0)
+    bias_part = jnp.stack([query_value_bias[0], jnp.zeros((own,), bf16), query_value_bias[1]])
+    small = [out_bias, norm1_gain, norm1_bias, down_bias, norm2_gain, norm2_bias, up_bias]
+    small = jnp.concatenate(small)
+    direct = lax.axis_size("c") == 4 and members == 4 and own % 8 == 0
+    if direct:
+        count = small.shape[0]
+        padded = jnp.pad(small, (0, 16 * LANES - count)).reshape(16, LANES)
+        spread = lax.dynamic_update_slice(
+            jnp.zeros((3, width), f32), bias_part.astype(f32), (0, lax.axis_index(ALL) * own)
+        )
+        spread = lay_out(jnp.transpose(spread.reshape(3, members, cols), (1, 0, 2)))
+        wq = jnp.transpose(qkv_weight.astype(f32).reshape(own, 3, members, cols), (2, 0, 1, 3))
+        wq = jnp.concatenate([lay_out(wq), spread[:, None], jnp.zeros((members, 7, heads * SLOT), f32)], axis=1)
+        mats = (out_weight, up_weight, down_weight)
+        x, tok, og, w_own, qkv, res, ctx, *full = front(
+            rand_flat, tokens[0], out_grad[0], wq, mats, padded, heads
+        )
+        x, tok = x.reshape(-1, width), tok.reshape(-1, width)
+        w_own = w_own.reshape(width, -1)
+        w_out, w_up, w_down = (a.reshape(-1, a.shape[-1]) for a in full[:3])
+        small = full[3].reshape(devices, -1)[:, :count].astype(f32)
+    else:
+        tok = move(tokens[0])
+        og = move(out_grad[0])
+        x = lax.all_gather(tok, GROUP, axis=0, tiled=True)
+        mats = (qkv_weight, out_weight, up_weight, down_weight)
+        w_qkv, w_out, w_up, w_down = (lax.all_gather(a, ALL, axis=0, tiled=True) for a in mats)
+        small = lax.all_gather(small, ALL, axis=0).astype(f32)
+        w_own = lax.dynamic_slice_in_dim(
+            w_qkv.reshape(width, 3, members, cols), group, 1, axis=2
+        ).reshape(width, 3, cols)
+        w_own = lay_out(w_own)
+        bias3 = lax.all_gather(bias_part, ALL, axis=1, tiled=True).astype(f32).reshape(3, members, cols)
+        b_own = lay_out(lax.dynamic_slice_in_dim(bias3, group, 1, axis=1).reshape(1, 3, cols))
+        qkv, res, ctx_send = attend(rand_flat, x, w_own, b_own, members, heads)
+        ctx = lax.all_to_all(ctx_send, GROUP, split_axis=0, concat_axis=0, tiled=True)
+    vecs = jnp.transpose(small[:, : 6 * own].reshape(devices, 6, own), (1, 0, 2)).reshape(6, width)
+    bias_up = small[:, 6 * own :].reshape(1, -1)
+    chain_vecs = jnp.concatenate([vecs, jnp.zeros((2, width), f32)], axis=0)
     out, dres1, dctx_send, mix, hid, act, dpre, dffn, dproj, gvec, gbu = chain(
         ctx, tok, og, w_out, w_up, w_down, chain_vecs, bias_up
     )

time: 643 us -> 494 us (0.77); the launches traced: 641 us -> 485 us
  Pallas kernels: 507 us -> 395 us
  local copies, waits for them, and re-layouts: 52.8 us -> 24.8 us
  waiting for transfers between devices: 15 us -> 0.01 us
    pallas_call x2 -> x1, Pallas kernels: 237 us -> 177 us  [front(): pl.pallas_call(partial(front_kernel, heads, randoms), out_shape=tuple(out...]
    pallas_call x1, Pallas kernels: 95.6 us -> 43.7 us  [attend_back(): pl.pallas_call(partial(attend_back_kernel, heads, randoms), out_shape=(ja...]
    all_to_all x1 -> x0, waiting for transfers between devices: 15 us -> none  [per_device(): lax.all_to_all(ctx_send, GROUP, split_axis=0, concat_axis=0, tiled=True)]
    another operation x5 -> x2, local copies, waits for them, and re-layouts: 10.2 us -> 0.17 us  [the longest x1 0.09 us: per_device(): spread[:, None]]
    dynamic_slice x3 -> x0, local copies, waits for them, and re-layouts: 9.47 us -> none  [the longest x2 6.82 us: per_device(): lax.dynamic_slice_in_dim(w_qkv.reshape(width, 3, members, cols), group, 1...]
  transfers between devices with their start and end apart: 4 -> 3, of which waited for: 1 -> 0; matrix products, arithmetic and copies ran while one was open for 9% -> 6% of each run, Pallas kernels for 24% -> 0%
where the time goes in v4:
time: 494 us; the launch traced here: 485 us
  Pallas kernels  395 us (80%)
  matrix products  38.9 us (8%)
  local copies, waits for them, and re-layouts  24.8 us (5%)
  starting transfers between devices  17.9 us (4%)
  other arithmetic  6 us (1%)
    pallas_call x1, Pallas kernels, front(): pl.pallas_call(partial(front_kernel, heads, randoms), out_shape=tuple(out...  177 us
    pallas_call x1, Pallas kernels, scatter(): pl.pallas_call(scatter_kernel, out_shape=tuple(outs), in_specs=[hbm] * 7,...  119 us
    pallas_call x1, Pallas kernels, chain(): pl.pallas_call(partial(chain_kernel, groups), grid=(rows // ROWS,), out_s...  55.4 us
    pallas_call x1, Pallas kernels, attend_back(): pl.pallas_call(partial(attend_back_kernel, heads, randoms), out_shape=(ja...  43.7 us
    dot_general x4, matrix products, dot_tn(): return lax.dot_general(a, b, TN, preferred_element_type=f32)  31.6 us
    ppermute x2, starting transfers between devices, move(): return lax.ppermute(a, ('core', 'zh'), swap)  14.2 us
  transfers between devices with their start and end apart: 3, of which 0 were waited for; matrix products, arithmetic and copies ran while one was open for 6% of the time, Pallas kernels for 0%

profile of v4, /device:TPU:0, one launch (start us, length us, event | category | flops | bytes accessed | tf_op | source)
XLA Modules:
  0.0 484.5 jit_solution(3043290777231042712)
XLA Ops:
  0.7 0.7 copy.57
  2.1 1.1 reshape.268
  6.3 0.8 maximum_maximum_fusion.refs_3_
  7.4 0.8 reshape.232.refs_0_.rand_ref
  8.2 177.2 %front.1 = (bf16[4,4,256,768]{3,2,1,0:T(8,128)(2,1)}, bf16[4,256,768]{2,1,0:T(8,128)(2,1)}, bf16[1024,768]{1,0:T(8,128)(2,1)}, bf16[2,2,2,2,48,768]{5,4,3,2,1,0:...) custom-call(s32[558]{0:T(1024)} %reshape.232.refs_0_.rand_ref, ...), custom_call_target="tpu_custom_call" | custom-call | tf_op jit(solution)/shard_map/front/pallas_call | solution.py:886
  185.4 0.9 copy.56
  186.6 0.7 reshape.247.bu_ref
  188.2 55.4 %chain.1 = (bf16[1024,768]{1,0:T(8,128)(2,1)}, f32[1024,768]{1,0:T(8,128)}, bf16[4,4,384,128]{3,2,1,0:T(8,128)(2,1)}, bf16[1024,768]{1,0:T(8,128)(2,1)}, bf16[10...) custom-call(bf16[4,4,384,128]{3,2,1,0:T(8,128)(2,1)} %get-tuple-elem, ...), custom_call_target="tpu_custom_call" | custom-call | tf_op jit(solution)/shard_map/chain/pallas_call | solution.py:467
  243.6 3.7 all-to-all-start
  247.3 13.6 %collective-permute-start.1 = (bf16[1024,768]{1,0:T(8,128)(2,1)}, bf16[1024,768]{1,0:T(8,128)(2,1)}, u32[]{:S(2)}, u32[]{:S(2)}) collective-permute-start(bf16[1024,768]{1,0:T(8,128)(2,1)} %get-tuple-element.51), channel_id=1, source_target_pairs={{0,0},{2,4},{4,2},{6,6},{1,1},{3,5},{5,3},{7,7},{8,8},{10,12},{12,... | collective-permute-start | bytes 4718600 | tf_op jit(solution)/shard_map/ppermute | solution.py:1154
  260.9 9.9 %convolution_convert_fusion.2 = bf16[3072,768]{1,0:T(8,128)(2,1)} fusion(bf16[1024,3072]{1,0:T(8,128)(2,1)} %get-tuple-element.52, bf16[1024,768]{1,0:T(8,128)(2,1)S(1)} %copy-done.17), kind=kOutput, calls=%fused_computation.2 | convolution fusion | flops 4834197504 | bytes 12582912 | tf_op jit(solution)/shard_map/dot_general | solution.py:42
  270.8 1.4 convolution_convert_fusion.4
  272.4 0.9 slice_reduce_fusion.2
  273.5 1.1 pad_maximum_fusion
  274.6 0.7 copy-done.14
  275.3 9.6 %convolution_convert_fusion.1 = bf16[768,3072]{1,0:T(8,128)(2,1)} fusion(bf16[1024,768]{1,0:T(8,128)(2,1)S(1)} %copy-done.14, bf16[1024,3072]{1,0:T(8,128)(2,1)} %get-tuple-element.55), kind=kOutput, calls=%fused_computation.1 | convolution fusion | flops 4834197504 | bytes 12582912 | tf_op jit(solution)/shard_map/dot_general | solution.py:42
  284.9 1.1 copy-done
  286.1 43.7 %attend_back.1 = (bf16[4096,768]{1,0:T(8,128)(2,1)}, f32[8,768]{1,0:T(8,128)}) custom-call(s32[558]{0:T(1024)} %reshape.232.refs_0_.rand_ref, bf16[64,64,768]{2,1,0:T(8,128)(2,1)} %get-tuple-element.58.qkv_ref, f32[3,4096,128]{2,1,0:T(8,128)} %get-tuple-element.59.res_ref, bf16[4,4,384,128]{3,2,1,0:T(8,128)(2,1)} %copy-done), custom_call_target="tpu_custom_call" | custom-call | tf_op jit(solution)/shard_map/attend_back/pallas_call | solution.py:304
  329.8 0.8 slice_reduce_fusion.3
  331.3 0.7 reshape.254.refs_3_
  332.0 10.7 %convolution_convert_fusion.3 = bf16[768,768]{1,0:T(8,128)(2,1)} fusion(bf16[4096,768]{1,0:T(8,128)(2,1)} %bitcast.108, bf16[4096,768]{1,0:T(8,128)(2,1)} %get-tuple-element.65), kind=kOutput, calls=%fused_computation.4 | convolution fusion | flops 4832428032 | bytes 13762560 | tf_op jit(solution)/shard_map/dot_general | solution.py:42
  342.7 7.3 %convolution_convert_fusion = bf16[4096,768]{1,0:T(8,128)(2,1)} fusion(bf16[4096,768]{1,0:T(8,128)(2,1)S(1)} %bitcast.110, bf16[768,768]{1,0:T(8,128)(2,1)S(1)} %bitcast.111), kind=kOutput, calls=%fused_computation | convolution fusion | flops 4834983936 | bytes 13762560 | tf_op jit(solution)/shard_map/dot_general | solution.py:38
  349.9 119.1 %scatter.1 = (f32[96,768]{1,0:T(8,128)}, f32[24,3072]{1,0:T(8,128)}, f32[24,768]{1,0:T(8,128)}, f32[8,128]{1,0:T(8,128)}, f32[4,24,768]{2,1,0:T(8,128)}, /*index=5*/bf16[4,256,768]{2,1,0:T(8,128)(2,1)}) custom-call(bf16[2,2,2,384,768]{4,3,2,1,0:T(8,128)(2,1)} %bitcast.84, bf16[2,2,2,96,3072]{4,3,2,1,0:T(8,128)(2,1)} %bitcast.85, ...), custom_call_target="tpu_custom_call" | custom-call | tf_op jit(solution)/shard_map/scatter/pallas_call | solution.py:1114
  469.1 1.3 slice.143
  471.0 1.5 fusion.5
  473.2 1.2 reshape.260
  474.4 1.4 fusion.2
  476.5 0.9 reshape.261
  477.4 1.9 bitcast_convert_fusion
  479.3 2.7 copy.65
  482.7 0.7 copy.67
  483.4 0.7 copy.68
  (107 shorter events, 8.6 us)
Async XLA Ops:
  0.6 3.2 copy-start.6
  0.7 3.2 copy-start.12
  0.7 3.2 copy-start.11
  0.7 3.2 copy-start.10
  0.7 3.2 copy-start.13
  0.7 3.2 copy-start.9
  0.7 3.2 copy-start.8
  0.7 3.2 copy-start.7
  1.5 5.8 %collective-permute-start = (s32[3,62,3]{1,2,0:T(4,128)S(1)}, s32[3,62,3]{1,2,0:T(4,128)S(1)}, u32[]{:S(2)}, u32[]{:S(2)}) collective-permute-start(s32[3,62,3]{1,2,0:T(4,128)S(1)} %bitcast.104), channel_id=1, source_target_pairs={{0,0},{2,4},{4,2},{6,6},{1,1},{3,5},{5,3},{7,7},{8,8},{10,12},{12,... | collective-permute-start | bytes 6704 | tf_op jit(solution)/shard_map/ppermute | solution.py:1154
  243.6 17.3 %copy-start.17 = (bf16[1024,768]{1,0:T(8,128)(2,1)S(1)}, bf16[1024,768]{1,0:T(8,128)(2,1)}, u32[]{:S(2)}) copy-start(bf16[1024,768]{1,0:T(8,128)(2,1)} %get-tuple-element.53) | copy-start | bytes 4718596
  243.6 41.3 %all-to-all-start = ((bf16[4,4,384,128]{3,2,1,0:T(8,128)(2,1)}), bf16[4,4,384,128]{3,2,1,0:T(8,128)(2,1)S(1)}, u32[]{:S(2)}, u32[]{:S(2)}) async-start(bf16[4,4,384,128]{3,2,1,0:T(8,128)(2,1)} %get-tuple-element.60), calls=%async_computation | async-start | bytes 3145728 | tf_op jit(solution)/shard_map/all_to_all | solution.py:1213
  247.3 37.6 %collective-permute-start.1 = (bf16[1024,768]{1,0:T(8,128)(2,1)}, bf16[1024,768]{1,0:T(8,128)(2,1)}, u32[]{:S(2)}, u32[]{:S(2)}) collective-permute-start(bf16[1024,768]{1,0:T(8,128)(2,1)} %get-tuple-element.51), channel_id=1, source_target_pairs={{0,0},{2,4},{4,2},{6,6},{1,1},{3,5},{5,3},{7,7},{8,8},{10,12},{12,... | collective-permute-start | bytes 4718600 | tf_op jit(solution)/shard_map/ppermute | solution.py:1154
  260.9 9.9 %copy-start.15 = (bf16[1024,768]{1,0:T(8,128)(2,1)S(1)}, bf16[1024,768]{1,0:T(8,128)(2,1)}, u32[]{:S(2)}) copy-start(bf16[1024,768]{1,0:T(8,128)(2,1)} %get-tuple-element.56) | copy-start | bytes 4718596
  260.9 9.9 %copy-start.16 = (bf16[1024,768]{1,0:T(8,128)(2,1)S(1)}, bf16[1024,768]{1,0:T(8,128)(2,1)}, u32[]{:S(2)}) copy-start(bf16[1024,768]{1,0:T(8,128)(2,1)} %get-tuple-element.57) | copy-start | bytes 4718596
  272.2 1.1 copy-start.5
  273.5 1.8 copy-start.14
  284.9 1.1 copy-start
  331.3 11.4 %slice-start = ((s8[6291456]{0:T(1024)(128)(4,1)}), s8[2097152]{0:T(1024)(128)(4,1)S(1)}, s32[]{:S(2)}) async-start(s8[6291456]{0:T(1024)(128)(4,1)} %bitcast.109), calls=%async_computation.1 | async-start | bytes 4194304
  332.0 10.7 %slice-start.1 = ((s8[6291456]{0:T(1024)(128)(4,1)}), s8[4194304]{0:T(1024)(128)(4,1)S(1)}, s32[]{:S(2)}) async-start(s8[6291456]{0:T(1024)(128)(4,1)} %bitcast.109), calls=%async_computation.2 | async-start | bytes 8388608
  332.0 10.7 %copy-start.18 = (bf16[2,2,2,2,48,768]{5,4,3,2,1,0:T(8,128)(2,1)S(1)}, bf16[2,2,2,2,48,768]{5,4,3,2,1,0:T(8,128)(2,1)}, u32[]{:S(2)}) copy-start(bf16[2,2,2,2,48,768]{5,4,3,2,1,0:T(8,128)(2,1)} %get-tuple-element.66) | copy-start | bytes 3538948
  474.4 3.0 copy-start.1
  479.3 2.7 copy-start.4
  479.3 3.4 copy-start.3
  479.3 4.1 copy-start.2
